TPU v7x, 128 devices: a whole 4x4x4 slice. The times are simulated.
128 devices in a mesh: section: 2 (over core), dp: 64 (over x, y, z).
Axes of the slice: x: 4, y: 4, z: 4, core: 2. Of those that a mesh axis runs over, the one named last changes fastest.
Arguments:
- inputs: bfloat16 [2, 4096, 1088], P(None, 'dp'), may hold values from -6 to 6
- cotangent: bfloat16 [2, 4096, 1088], P(None, 'dp'), may hold values from -6 to 6
- lengths: int32 [2, 64, 4], P(None, 'dp'), may hold values from 1 to 32, as said below
- vectors: bfloat16 [2, 1088, 8], P('section', 'dp'), may hold values from -1.5 to 1.5, as said below
- qkv_weight: bfloat16 [2, 1088, 3264], P('section', 'dp'), may hold values from -0.1875 to 0.1875
- out_weight: bfloat16 [2, 1088, 1088], P('section', 'dp'), may hold values from -0.75 to 0.75
- up_weight: bfloat16 [2, 1088, 4352], P('section', 'dp'), may hold values from -0.1875 to 0.1875
- up_bias: bfloat16 [2, 4352], P('section', 'dp'), may hold values from -1.5 to 1.5
- down_weight: bfloat16 [2, 4352, 1088], P('section', 'dp'), may hold values from -0.09375 to 0.09375
Outputs:
- acts_out: bfloat16 [2, 2, 4096, 1088], P('section', None, 'dp')
- grad_in: bfloat16 [2, 2, 4096, 1088], P('section', None, 'dp')
- grad_vectors: float32 [2, 1088, 8], P('section', 'dp')
- grad_qkv: float32 [2, 1088, 3264], P('section', 'dp')
- grad_out: float32 [2, 1088, 1088], P('section', 'dp')
- grad_up: float32 [2, 1088, 4352], P('section', 'dp')
- grad_up_bias: float32 [2, 4352], P('section', 'dp')
- grad_down: float32 [2, 4352, 1088], P('section', 'dp')
Inputs may be any that keep to these rules, and one draw needn't show every extreme that they name: The 4 lengths of each block sum to 64, and exactly one of them is 32. `vectors`: columns 0 and 5 lie in 0.6 to 1.4.
All inputs are finite; a program needn't handle non-finite values.
Results may differ from a plain program's by a relative error of at most 0.017.
Values may be sent and summed in bfloat16 or wider, within the bound.
No kernel may reach another device: no remote copies, remote signals or barrier semaphores. Data moves between devices by JAX's collectives and lax.ppermute only.
A program may use at most 192 MiB of HBM per device.

v0:
```python
from functools import partial

import jax
import jax.numpy as jnp
from jax import lax
from jax.sharding import PartitionSpec as P

HEADS = 17
HDIM = 64


NORM_EPSILON = 1e-05
SCORE_SCALE = 0.125


def shifted(block, axis, distance):
    devices = range(lax.axis_size(axis))
    route = [(i - distance, i) for i in devices if i - distance in devices]
    return lax.ppermute(block, axis, route)


def matmul(left_side, right_side):
    return jnp.dot(left_side, right_side, preferred_element_type=jnp.float32)


def inner_rows(left_side, right_side):
    return lax.dot_general(
        left_side, right_side, (((0,), (0,)), ((), ())), preferred_element_type=jnp.float32
    )


def outer_cols(left_side, right_side):
    return lax.dot_general(
        left_side, right_side, (((1,), (1,)), ((), ())), preferred_element_type=jnp.float32
    )


def gelu_tanh(features):
    return jax.nn.gelu(features, approximate=True)


def norm_parts(features):
    row_mean = jnp.mean(features, axis=-1, keepdims=True)
    centred = features - row_mean
    inverse = lax.rsqrt(jnp.mean(centred * centred, axis=-1, keepdims=True) + NORM_EPSILON)
    return (centred * inverse, inverse)


def norm_back(gradient, normed, inverse, gain_vec):
    gain_grad = jnp.sum(gradient * normed, axis=0)
    bias_grad = jnp.sum(gradient, axis=0)
    scaled = gradient * gain_vec
    centred = scaled - jnp.mean(scaled, axis=-1, keepdims=True)
    centred = centred - normed * jnp.mean(scaled * normed, axis=-1, keepdims=True)
    return (inverse * centred, gain_grad, bias_grad)


def segment_ids(seq_lengths, row_count):
    boundaries = jnp.cumsum(seq_lengths)
    places = jnp.arange(row_count, dtype=jnp.int32)
    return jnp.sum((places[:, None] >= boundaries[None, :]).astype(jnp.int32), axis=1)


def allowed_pairs(segment):
    places = jnp.arange(segment.shape[0], dtype=jnp.int32)
    return (segment[:, None] == segment[None, :]) & (places[:, None] >= places[None, :])


def split_heads(packed):
    row_count = packed.shape[0]
    feature_count = packed.shape[1] // 3
    return [
        packed[:, column_block * feature_count : (column_block + 1) * feature_count].reshape(
            row_count, HEADS, HDIM
        )
        for column_block in range(3)
    ]


def attention(packed, segment):
    queries, keys_heads, values_heads = split_heads(packed)
    allowed = allowed_pairs(segment)[None]
    scores = (
        jnp.einsum("qhd,khd->hqk", queries, keys_heads, preferred_element_type=jnp.float32)
        * SCORE_SCALE
    )
    scores = jnp.where(allowed, scores, -1e30)
    highest = jnp.max(scores, axis=-1, keepdims=True)
    exponent = jnp.exp(scores - highest)
    totals = jnp.sum(exponent, axis=-1, keepdims=True)
    soft_weights = (exponent / totals).astype(jnp.bfloat16)
    mixed_heads = jnp.einsum(
        "hqk,khd->qhd", soft_weights, values_heads, preferred_element_type=jnp.float32
    )
    return (
        mixed_heads.reshape(packed.shape[0], -1).astype(jnp.bfloat16),
        highest + jnp.log(totals),
    )


def attention_back(packed, segment, log_totals, grad_mixed):
    queries, keys_heads, values_heads = split_heads(packed)
    row_count = packed.shape[0]
    allowed = allowed_pairs(segment)[None]
    scores = (
        jnp.einsum("qhd,khd->hqk", queries, keys_heads, preferred_element_type=jnp.float32)
        * SCORE_SCALE
    )
    soft_weights = jnp.where(allowed, jnp.exp(scores - log_totals), 0.0)
    grad_heads = grad_mixed.reshape(row_count, HEADS, HDIM)
    grad_soft = jnp.einsum(
        "qhd,khd->hqk", grad_heads, values_heads, preferred_element_type=jnp.float32
    )
    grad_values = jnp.einsum(
        "hqk,qhd->khd",
        soft_weights.astype(jnp.bfloat16),
        grad_heads,
        preferred_element_type=jnp.float32,
    )
    centre = jnp.sum(grad_soft * soft_weights, axis=-1, keepdims=True)
    grad_scores = (soft_weights * (grad_soft - centre)).astype(jnp.bfloat16)
    grad_queries = (
        jnp.einsum("hqk,khd->qhd", grad_scores, keys_heads, preferred_element_type=jnp.float32)
        * SCORE_SCALE
    )
    grad_keys = (
        jnp.einsum("hqk,qhd->khd", grad_scores, queries, preferred_element_type=jnp.float32)
        * SCORE_SCALE
    )
    pieces = [
        piece.reshape(row_count, -1).astype(jnp.bfloat16)
        for piece in (grad_queries, grad_keys, grad_values)
    ]
    return jnp.concatenate(pieces, axis=1)


def layer_forward(features, segment, weights):
    qkv_weight, out_weight, up_weight, down_weight, vectors, up_bias = weights
    columns = vectors.astype(jnp.float32)
    normed_first, inverse_first = norm_parts(features)
    entry = (normed_first * columns[:, 0] + columns[:, 1]).astype(jnp.bfloat16)
    packed_bias = jnp.concatenate([columns[:, 2], jnp.zeros_like(columns[:, 2]), columns[:, 3]])
    packed = (matmul(entry, qkv_weight) + packed_bias).astype(jnp.bfloat16)
    mixed_rows, log_totals = attention(packed, segment)
    middle = features + matmul(mixed_rows, out_weight) + columns[:, 4]
    normed_second, inverse_second = norm_parts(middle)
    second = (normed_second * columns[:, 5] + columns[:, 6]).astype(jnp.bfloat16)
    hidden = matmul(second, up_weight) + up_bias.astype(jnp.float32)
    active = gelu_tanh(hidden).astype(jnp.bfloat16)
    result = middle + matmul(active, down_weight) + columns[:, 7]
    kept = (
        normed_first,
        inverse_first,
        entry,
        packed,
        mixed_rows,
        log_totals,
        normed_second,
        inverse_second,
        second,
        hidden,
        active,
    )
    return (result, kept)


def empty_kept(row_count, feature_count, hidden_count):
    return (
        jnp.zeros((row_count, feature_count), jnp.float32),
        jnp.zeros((row_count, 1), jnp.float32),
        jnp.zeros((row_count, feature_count), jnp.bfloat16),
        jnp.zeros((row_count, 3 * feature_count), jnp.bfloat16),
        jnp.zeros((row_count, feature_count), jnp.bfloat16),
        jnp.zeros((HEADS, row_count, 1), jnp.float32),
        jnp.zeros((row_count, feature_count), jnp.float32),
        jnp.zeros((row_count, 1), jnp.float32),
        jnp.zeros((row_count, feature_count), jnp.bfloat16),
        jnp.zeros((row_count, hidden_count), jnp.float32),
        jnp.zeros((row_count, hidden_count), jnp.bfloat16),
    )


def empty_factors(row_count, feature_count, hidden_count):
    return (
        jnp.zeros((row_count, feature_count), jnp.bfloat16),
        jnp.zeros((row_count, 3 * feature_count), jnp.bfloat16),
        jnp.zeros((row_count, feature_count), jnp.bfloat16),
        jnp.zeros((row_count, feature_count), jnp.bfloat16),
        jnp.zeros((row_count, feature_count), jnp.bfloat16),
        jnp.zeros((row_count, hidden_count), jnp.bfloat16),
        jnp.zeros((row_count, hidden_count), jnp.bfloat16),
        jnp.zeros((row_count, feature_count), jnp.bfloat16),
    )


def layer_backward(features, segment, weights, grad_out, starting, kept):
    qkv_weight, out_weight, up_weight, down_weight, vectors, up_bias = weights
    columns = vectors.astype(jnp.float32)
    (
        normed_first,
        inverse_first,
        entry,
        packed,
        mixed_rows,
        log_totals,
        normed_second,
        inverse_second,
        second,
        hidden,
        active,
    ) = kept
    grad_branch = grad_out.astype(jnp.bfloat16)
    grad_down_bias = jnp.sum(grad_branch.astype(jnp.float32), axis=0)
    grad_active = outer_cols(grad_branch, down_weight)
    grad_hidden = jax.vjp(gelu_tanh, hidden)[1](grad_active)[0].astype(jnp.bfloat16)
    grad_up_bias = jnp.sum(grad_hidden.astype(jnp.float32), axis=0)
    grad_second = outer_cols(grad_hidden, up_weight)
    grad_norm_second, grad_gain_second, grad_bias_second = norm_back(
        grad_second, normed_second, inverse_second, columns[:, 5]
    )
    grad_middle = grad_out + grad_norm_second
    grad_attn = grad_middle.astype(jnp.bfloat16)
    grad_out_bias = jnp.sum(grad_attn.astype(jnp.float32), axis=0)
    grad_mixed = outer_cols(grad_attn, out_weight).astype(jnp.bfloat16)
    grad_packed = attention_back(packed, segment, log_totals, grad_mixed)
    packed_sums = jnp.sum(grad_packed.astype(jnp.float32), axis=0)
    feature_count = features.shape[1]
    grad_entry = outer_cols(grad_packed, qkv_weight)
    grad_norm_first, grad_gain_first, grad_bias_first = norm_back(
        grad_entry, normed_first, inverse_first, columns[:, 0]
    )
    grad_features = grad_middle + grad_norm_first
    grad_columns = jnp.stack(
        [
            grad_gain_first,
            grad_bias_first,
            packed_sums[:feature_count],
            packed_sums[2 * feature_count :],
            grad_out_bias,
            grad_gain_second,
            grad_bias_second,
            grad_down_bias,
        ],
        axis=1,
    )
    factors = (entry, grad_packed, mixed_rows, grad_attn, second, grad_hidden, active, grad_branch)
    small = (starting[0] + grad_columns, starting[1] + grad_up_bias)
    return (grad_features, factors, small)


def forward_run(entering, segment, weights):
    result, kept = layer_forward(entering.astype(jnp.float32), segment, weights)
    return (result.astype(jnp.bfloat16), kept)


def forward_skip(entering, segment, hidden_count):
    return (
        jnp.zeros_like(entering),
        empty_kept(entering.shape[0], entering.shape[1], hidden_count),
    )


def backward_stored(kept_in, segment, grad_out, starting, kept, weights):
    grad_features, factors, small = layer_backward(
        kept_in.astype(jnp.float32), segment, weights, grad_out.astype(jnp.float32), starting, kept
    )
    return (grad_features.astype(jnp.bfloat16), factors, small)


def backward_skip(kept_in, segment, grad_out, starting, kept, hidden_count):
    return (
        jnp.zeros_like(kept_in),
        empty_factors(kept_in.shape[0], kept_in.shape[1], hidden_count),
        starting,
    )


def body(
    inputs, cotangent, lengths, vectors, qkv_weight, out_weight, up_weight, up_bias, down_weight
):
    section_index = lax.axis_index("section")
    micro_count, row_count, feature_count = inputs.shape
    shards = (qkv_weight[0], out_weight[0], up_weight[0], down_weight[0], vectors[0], up_bias[0])
    weights = (
        lax.all_gather(shards[0], "dp", axis=0, tiled=True),
        lax.all_gather(shards[1], "dp", axis=0, tiled=True),
        lax.all_gather(shards[2], "dp", axis=0, tiled=True),
        lax.all_gather(shards[3], "dp", axis=0, tiled=True),
        lax.all_gather(shards[4], "dp", axis=0, tiled=True),
        lax.all_gather(shards[5], "dp", axis=0, tiled=True),
    )
    hidden_count = weights[2].shape[1]
    segments = jnp.stack(
        [segment_ids(lengths[micro_index, 0], row_count) for micro_index in range(micro_count)]
    )
    layer_out = jnp.zeros((micro_count, row_count, feature_count), jnp.bfloat16)
    layer_in = jnp.zeros_like(layer_out)
    stored = tuple(
        (
            jnp.zeros((micro_count,) + piece.shape, piece.dtype)
            for piece in empty_kept(row_count, feature_count, hidden_count)
        )
    )
    arrived = jnp.zeros((row_count, feature_count), jnp.bfloat16)
    for step_index in range(micro_count + 1):
        slot_raw = step_index - section_index
        active_step = (slot_raw >= 0) & (slot_raw < micro_count)
        slot_index = jnp.clip(slot_raw, 0, micro_count - 1)
        entering = jnp.where(section_index == 0, inputs[min(step_index, micro_count - 1)], arrived)
        segment = lax.dynamic_index_in_dim(segments, slot_index, 0, keepdims=False)
        leaving, kept = lax.cond(
            active_step,
            partial(forward_run, weights=weights),
            partial(forward_skip, hidden_count=hidden_count),
            entering,
            segment,
        )
        layer_out = jnp.where(
            active_step,
            lax.dynamic_update_index_in_dim(layer_out, leaving, slot_index, 0),
            layer_out,
        )
        layer_in = jnp.where(
            active_step,
            lax.dynamic_update_index_in_dim(layer_in, entering, slot_index, 0),
            layer_in,
        )
        stored = tuple(
            (
                jnp.where(
                    active_step, lax.dynamic_update_index_in_dim(whole, piece, slot_index, 0), whole
                )
                for whole, piece in zip(stored, kept)
            )
        )
        if step_index < micro_count:
            arrived = shifted(leaving, "section", 1)
    small = (jnp.zeros((feature_count, 8), jnp.float32), jnp.zeros((hidden_count,), jnp.float32))
    factor_store = tuple(
        (
            jnp.zeros((micro_count,) + piece.shape, piece.dtype)
            for piece in empty_factors(row_count, feature_count, hidden_count)
        )
    )
    grads_in = jnp.zeros_like(layer_out)
    coming = jnp.zeros((row_count, feature_count), jnp.bfloat16)
    for step_index in range(micro_count + 1):
        slot_raw = step_index - (1 - section_index)
        active_step = (slot_raw >= 0) & (slot_raw < micro_count)
        slot_index = jnp.clip(slot_raw, 0, micro_count - 1)
        grad_out = jnp.where(
            section_index == 1, cotangent[min(step_index, micro_count - 1)], coming
        )
        kept_in = lax.dynamic_index_in_dim(layer_in, slot_index, 0, keepdims=False)
        segment = lax.dynamic_index_in_dim(segments, slot_index, 0, keepdims=False)
        kept = tuple(
            (lax.dynamic_index_in_dim(whole, slot_index, 0, keepdims=False) for whole in stored)
        )
        runner = partial(backward_stored, weights=weights)
        grad_back, factors, small = lax.cond(
            active_step,
            runner,
            partial(backward_skip, hidden_count=hidden_count),
            kept_in,
            segment,
            grad_out,
            small,
            kept,
        )
        grads_in = jnp.where(
            active_step,
            lax.dynamic_update_index_in_dim(grads_in, grad_back, slot_index, 0),
            grads_in,
        )
        factor_store = tuple(
            (
                jnp.where(
                    active_step, lax.dynamic_update_index_in_dim(whole, piece, slot_index, 0), whole
                )
                for whole, piece in zip(factor_store, factors)
            )
        )
        if step_index < micro_count:
            coming = shifted(grad_back, "section", -1)
    flat = [whole.reshape(micro_count * row_count, whole.shape[2]) for whole in factor_store]
    (
        entry_all,
        gpacked_all,
        mixed_all,
        gattn_all,
        second_all,
        ghidden_all,
        active_all,
        gbranch_all,
    ) = flat
    grad_columns_all, grad_up_bias_all = small
    totals = (
        inner_rows(entry_all, gpacked_all),
        inner_rows(mixed_all, gattn_all),
        inner_rows(second_all, ghidden_all),
        inner_rows(active_all, gbranch_all),
        grad_columns_all,
        grad_up_bias_all,
    )
    grad_qkv, grad_outproj, grad_up, grad_down, grad_columns, grad_up_bias = (
        lax.psum_scatter(totals[0], "dp", scatter_dimension=0, tiled=True),
        lax.psum_scatter(totals[1], "dp", scatter_dimension=0, tiled=True),
        lax.psum_scatter(totals[2], "dp", scatter_dimension=0, tiled=True),
        lax.psum_scatter(totals[3], "dp", scatter_dimension=0, tiled=True),
        lax.psum_scatter(totals[4], "dp", scatter_dimension=0, tiled=True),
        lax.psum_scatter(totals[5], "dp", scatter_dimension=0, tiled=True),
    )
    return (
        layer_out[None],
        grads_in[None],
        grad_columns[None],
        grad_qkv[None],
        grad_outproj[None],
        grad_up[None],
        grad_up_bias[None],
        grad_down[None],
    )


def solution(mesh):
    in_specs = (
        P(None, "dp", None),
        P(None, "dp", None),
        P(None, "dp", None),
        P("section", "dp", None),
        P("section", "dp", None),
        P("section", "dp", None),
        P("section", "dp", None),
        P("section", "dp"),
        P("section", "dp", None),
    )
    out_specs = (
        P("section", None, "dp", None),
        P("section", None, "dp", None),
        P("section", "dp", None),
        P("section", "dp", None),
        P("section", "dp", None),
        P("section", "dp", None),
        P("section", "dp"),
        P("section", "dp", None),
    )
    return jax.shard_map(body, mesh=mesh, in_specs=in_specs, out_specs=out_specs, check_vma=False)
```

profile of v0, /device:TPU:0, one launch (start us, length us, event | category | flops | bytes accessed | tf_op | source)
XLA Modules:
  0.0 2488.6 jit_solution(5599289744860557981)
XLA Ops:
  14.3 183.0 %all-gather = bf16[1,1088,8]{2,0,1:T(2,128)(2,1)S(1)} all-gather(bf16[1,17,8]{2,0,1:T(2,128)(2,1)S(1)} %copy.339), channel_id=2, replica_groups=mesh['section'=2,'dp'=64] {'dp'}, dimensions={1}, use_global_device_ids=true | all-gather | bytes 17680 | tf_op jit(solution)/shard_map/all_gather | solution.py:289
  199.6 344.1 %all-reduce = bf16[4352]{0:T(1024)(128)(2,1)S(1)} all-reduce(bf16[4352]{0:T(1024)(128)(2,1)S(1)} %dynamic-update-slice.65), channel_id=6, replica_groups=mesh['section'=2,'dp'=64] {'dp'}, use_global_device_ids=true, to_apply=%add | all-reduce | flops 4352 | bytes 17408 | tf_op jit(solution)/shard_map/all_gather | solution.py:290
  558.6 40.1 %copy.345 = bf16[1,4352,1088]{1,2,0:T(8,128)(2,1)} copy(bf16[1,4352,1088]{2,0,1:T(2,128)(2,1)} %all-gather.17.cloned.1.call-done) | data formatting | bytes 18939904 | tf_op jit(solution)/shard_map/all_gather | solution.py:288
  598.7 13.8 copy.429
  613.2 33.7 %conditional.6 = (bf16[64,1088]{1,0:T(8,128)(2,1)}, f32[64,1088]{1,0:T(8,128)}, bf16[64,1088]{1,0:T(8,128)(2,1)}, f32[64,1088]{1,0:T(8,128)}, bf16[64,1088]{1,0:...) conditional(s32[]{:T(128)} %convert_element_type.452, ...), branch_computations={%region_4.5_spmd, %region_5.12_spmd} | conditional | flops 1841860352 | bytes 73765472 | solution.py:311
  661.3 39.6 %conditional.7 = (bf16[64,1088]{1,0:T(8,128)(2,1)}, bf16[1,64,1088]{2,1,0:T(8,128)(2,1)}, f32[1,64,1088]{2,1,0:T(8,128)}, f32[1,64,1]{1,2,0:T(1,128)}, bf16[1,64...) conditional(s32[]{:T(128)} %convert_element_type.455, ...), branch_computations={%region_12.13_spmd, %region_13.20_spmd} | conditional | flops 1845133056 | bytes 75213840 | solution.py:311
  757.5 37.3 %collective-permute-done.2 = bf16[64,1088]{1,0:T(8,128)(2,1)S(1)} collective-permute-done((bf16[64,1088]{1,0:T(8,128)(2,1)}, bf16[64,1088]{1,0:T(8,128)(2,1)S(1)}, u32[]{:S(2)}, u32[]{:S(2)}) %collective-permute-start.2) | collective-permute-done | bytes 139296 | tf_op jit(solution)/shard_map/ppermute | solution.py:19
  794.9 28.3 %conditional.10 = (bf16[64,1088]{1,0:T(8,128)(2,1)}, f32[1088,8]{0,1:T(8,128)}, f32[4352]{0:T(1024)}, bf16[1,64,1088]{2,1,0:T(8,128)(2,1)}, bf16[1,64,1088]{2,1,...) conditional(s32[]{:T(128)} %convert_element_type.458, ...), branch_computations={%region_43.44_spmd, %region_44.58_spmd} | conditional | flops 1876461824 | bytes 132275688 | solution.py:360
  835.0 30.4 %conditional.11 = (f32[1088,8]{0,1:T(8,128)}, f32[4352]{0:T(1024)}, bf16[1,64,1088]{2,1,0:T(8,128)(2,1)}, bf16[1,64,1088]{2,1,0:T(8,128)(2,1)}, bf16[1,64,3264]{...) conditional(s32[]{:T(128)} %convert_element_type.459, ...), branch_computations={%region_58.59_spmd, %region_59.73_spmd} | conditional | flops 1876461824 | bytes 124180928 | solution.py:360
  888.2 506.7 %fusion.187 = (f32[24,3264]{1,0:T(8,128)S(1)}, f32[24,4352]{1,0:T(8,128)S(1)}) fusion(f32[1088,3264]{1,0:T(8,128)} %convolution_bitcast_fusion.2, f32[1088,4352]{1,0:T(8,128)} %convolution_bitcast_fusion.1), kind=kCustom, calls=%all-reduce-scatter.3 | all-reduce-scatter fusion | flops 11698177 | bytes 33876480
  1407.2 267.9 %fusion.2 = f32[80,1088]{1,0:T(8,128)S(1)} fusion(f32[4352,1088]{1,0:T(8,128)} %convolution_bitcast_fusion), kind=kCustom, calls=%all-reduce-scatter.2 | all-reduce-scatter fusion | flops 5570561 | bytes 19288576
  1692.7 11.0 collective-permute-start.13
  1709.8 10.6 collective-permute-start.15
  1761.6 13.1 collective-permute-start.43
  1776.6 11.1 collective-permute-start.8
  1804.8 12.0 collective-permute-start.45
  1824.0 40.6 %collective-permute-start.47 = (f32[80,1088]{1,0:T(8,128)S(1)}, f32[80,1088]{1,0:T(8,128)S(1)}, u32[]{:S(2)}, u32[]{:S(2)}) collective-permute-start(f32[80,1088]{1,0:T(8,128)S(1)} %fusion.2), channel_id=1, source_target_pairs={{0,6},{1,7},{2,8},{3,9},{4,10},{5,11},{6,12},{7,13},{8,14},{9,15},... | collective-permute-start | bytes 1044488
  1866.2 18.9 collective-permute-start.49
  1910.4 24.9 %collective-permute-start.28 = (f32[24,4352]{1,0:T(8,128)S(1)}, f32[24,4352]{1,0:T(8,128)}, u32[]{:S(2)}, u32[]{:S(2)}) collective-permute-start(f32[24,4352]{1,0:T(8,128)S(1)} %get-tuple-element.1751), channel_id=1, source_target_pairs={{0,6},{1,7},{2,8},{3,9},{4,10},{5,11},{6,12},{7,13},{8,14},{9,15},... | collective-permute-start | bytes 1253384
  1937.4 18.1 collective-permute-start.30
  1956.6 343.7 %all-reduce.10 = (f32[1088,8]{0,1:T(8,128)S(1)}, f32[4352]{0:T(1024)S(1)}) all-reduce(f32[1088,8]{0,1:T(8,128)} %get-tuple-element.1061, f32[4352]{0:T(1024)} %get-tuple-element.1080), channel_id=8, replica_groups=mesh['section'=2,'dp'=64] {'dp'}, use_global_device_ids=true, to_apply=%region_73.74.clone | all-reduce | flops 13056 | bytes 104448
  2312.7 62.4 %concatenate.27 = f32[465,3264]{1,0:T(8,128)} concatenate(f32[9,3264]{1,0:T(8,128)} %copy-done.158, f32[24,3264]{1,0:T(8,128)} %copy-done.138, f32[24,3264]{1,0:T(8,128)} %copy-done.137, f32[24,3264]{1,0:T(8,128)} %collective-permute-done.19, f32[24,3264]{1,0:T(8,128)} %collective-permute-done.18, f32[24,3264]{1,0:T(8,128)} %copy-done.136, f32[24,3264]{1,0:T(8,128)} %copy-done.135, ...), dimensions={0} | concatenate | bytes 12142080
  2395.2 18.4 concatenate.29
  2415.7 62.4 %concatenate.28 = f32[465,4352]{1,0:T(8,128)} concatenate(f32[9,4352]{1,0:T(8,128)S(1)} %copy-done.157, f32[24,4352]{1,0:T(8,128)} %collective-permute-done.40, f32[24,4352]{1,0:T(8,128)} %collective-permute-done.39, f32[24,4352]{1,0:T(8,128)} %collective-permute-done.38, f32[24,4352]{1,0:T(8,128)S(1)} %collective-permute-done.37, f32[24,4352]{1,0:T(8,128)S(1)} %collective-permute-done.36, ...), dimensions={0} | concatenate | bytes 16189440
  (798 shorter events, 442.0 us)
Async XLA Ops:
  7.2 538.5 %all-gather.13.cloned.1.call-start = ((), (), s32[]{:S(2)}) async-start(), calls=%async_computation.1 | async-start | bytes 5091840 | tf_op jit(solution)/shard_map/all_gather | solution.py:286
  8.8 539.7 %all-gather.11.cloned.1.call-start = ((), (), s32[]{:S(2)}) async-start(), calls=%async_computation | async-start | bytes 14709760 | tf_op jit(solution)/shard_map/all_gather | solution.py:285
  10.7 547.9 %all-gather.17.cloned.1.call-start = ((), (), s32[]{:S(2)}) async-start(), calls=%async_computation.3 | async-start | bytes 20367360 | tf_op jit(solution)/shard_map/all_gather | solution.py:288
  12.7 586.0 %all-gather.15.cloned.1.call-start = ((), (), s32[]{:S(2)}) async-start(), calls=%async_computation.2 | async-start | bytes 19235840 | tf_op jit(solution)/shard_map/all_gather | solution.py:287
  13.7 2466.5 %all-reduce.14.cloned.1.call-start = ((), (), s32[]{:S(2)}) async-start(), calls=%async_computation.4 | async-start | bytes 10027008
  745.3 49.5 %collective-permute-start.2 = (bf16[64,1088]{1,0:T(8,128)(2,1)}, bf16[64,1088]{1,0:T(8,128)(2,1)S(1)}, u32[]{:S(2)}, u32[]{:S(2)}) collective-permute-start(bf16[64,1088]{1,0:T(8,128)(2,1)} %get-tuple-element.1055), channel_id=1, source_target_pairs={{64,0},{65,1},{66,2},{67,3},{68,4},{69,5},{70,6},{71,7},{72,8},{73... | collective-permute-start | bytes 417800 | tf_op jit(solution)/shard_map/ppermute | solution.py:19
  1395.0 314.8 %collective-permute-start.10 = (f32[24,3264]{1,0:T(8,128)S(1)}, f32[24,3264]{1,0:T(8,128)S(1)}, u32[]{:S(2)}, u32[]{:S(2)}) collective-permute-start(f32[24,3264]{1,0:T(8,128)S(1)} %get-tuple-element.1750), channel_id=1, source_target_pairs={{0,7},{1,8},{2,9},{3,10},{4,11},{5,12},{6,13},{7,14},{8,15},{9,16}... | collective-permute-start | bytes 940040
  1396.3 324.1 %collective-permute-start.11 = (f32[24,3264]{1,0:T(8,128)S(1)}, f32[24,3264]{1,0:T(8,128)S(1)}, u32[]{:S(2)}, u32[]{:S(2)}) collective-permute-start(f32[24,3264]{1,0:T(8,128)S(1)} %get-tuple-element.1750), channel_id=1, source_target_pairs={{0,8},{1,9},{2,10},{3,11},{4,12},{5,13},{6,14},{7,15},{8,16},{9,17... | collective-permute-start | bytes 940040
  1759.0 65.0 %collective-permute-start.42 = (f32[80,1088]{1,0:T(8,128)S(1)}, f32[80,1088]{1,0:T(8,128)S(1)}, u32[]{:S(2)}, u32[]{:S(2)}) collective-permute-start(f32[80,1088]{1,0:T(8,128)S(1)} %fusion.2), channel_id=1, source_target_pairs={{0,1},{1,2},{2,3},{3,4},{4,5},{5,6},{6,7},{7,8},{8,9},{9,10},{10,1... | collective-permute-start | bytes 1044488
  1761.6 103.1 %collective-permute-start.43 = (f32[80,1088]{1,0:T(8,128)S(1)}, f32[80,1088]{1,0:T(8,128)S(1)}, u32[]{:S(2)}, u32[]{:S(2)}) collective-permute-start(f32[80,1088]{1,0:T(8,128)S(1)} %fusion.2), channel_id=1, source_target_pairs={{0,2},{1,3},{2,4},{3,5},{4,6},{5,7},{6,8},{7,9},{8,10},{9,11},{10,... | collective-permute-start | bytes 1044488
  1797.2 68.9 %collective-permute-start.44 = (f32[80,1088]{1,0:T(8,128)S(1)}, f32[80,1088]{1,0:T(8,128)S(1)}, u32[]{:S(2)}, u32[]{:S(2)}) collective-permute-start(f32[80,1088]{1,0:T(8,128)S(1)} %fusion.2), channel_id=1, source_target_pairs={{0,3},{1,4},{2,5},{3,6},{4,7},{5,8},{6,9},{7,10},{8,11},{9,12},{10... | collective-permute-start | bytes 1044488
  1804.8 80.2 %collective-permute-start.45 = (f32[80,1088]{1,0:T(8,128)S(1)}, f32[80,1088]{1,0:T(8,128)S(1)}, u32[]{:S(2)}, u32[]{:S(2)}) collective-permute-start(f32[80,1088]{1,0:T(8,128)S(1)} %fusion.2), channel_id=1, source_target_pairs={{0,4},{1,5},{2,6},{3,7},{4,8},{5,9},{6,10},{7,11},{8,12},{9,13},{1... | collective-permute-start | bytes 1044488
  1816.9 69.5 %collective-permute-start.46 = (f32[80,1088]{1,0:T(8,128)S(1)}, f32[80,1088]{1,0:T(8,128)S(1)}, u32[]{:S(2)}, u32[]{:S(2)}) collective-permute-start(f32[80,1088]{1,0:T(8,128)S(1)} %fusion.2), channel_id=1, source_target_pairs={{0,5},{1,6},{2,7},{3,8},{4,9},{5,10},{6,11},{7,12},{8,13},{9,14},{... | collective-permute-start | bytes 1044488
  1824.0 64.6 %collective-permute-start.47 = (f32[80,1088]{1,0:T(8,128)S(1)}, f32[80,1088]{1,0:T(8,128)S(1)}, u32[]{:S(2)}, u32[]{:S(2)}) collective-permute-start(f32[80,1088]{1,0:T(8,128)S(1)} %fusion.2), channel_id=1, source_target_pairs={{0,6},{1,7},{2,8},{3,9},{4,10},{5,11},{6,12},{7,13},{8,14},{9,15},... | collective-permute-start | bytes 1044488
  1899.0 402.5 %collective-permute-start.26 = (f32[24,4352]{1,0:T(8,128)S(1)}, f32[24,4352]{1,0:T(8,128)}, u32[]{:S(2)}, u32[]{:S(2)}) collective-permute-start(f32[24,4352]{1,0:T(8,128)S(1)} %get-tuple-element.1751), channel_id=1, source_target_pairs={{0,4},{1,5},{2,6},{3,7},{4,8},{5,9},{6,10},{7,11},{8,12},{9,13},{1... | collective-permute-start | bytes 1253384
  1906.9 396.7 %collective-permute-start.27 = (f32[24,4352]{1,0:T(8,128)S(1)}, f32[24,4352]{1,0:T(8,128)}, u32[]{:S(2)}, u32[]{:S(2)}) collective-permute-start(f32[24,4352]{1,0:T(8,128)S(1)} %get-tuple-element.1751), channel_id=1, source_target_pairs={{0,5},{1,6},{2,7},{3,8},{4,9},{5,10},{6,11},{7,12},{8,13},{9,14},{... | collective-permute-start | bytes 1253384
  1910.4 395.2 %collective-permute-start.28 = (f32[24,4352]{1,0:T(8,128)S(1)}, f32[24,4352]{1,0:T(8,128)}, u32[]{:S(2)}, u32[]{:S(2)}) collective-permute-start(f32[24,4352]{1,0:T(8,128)S(1)} %get-tuple-element.1751), channel_id=1, source_target_pairs={{0,6},{1,7},{2,8},{3,9},{4,10},{5,11},{6,12},{7,13},{8,14},{9,15},... | collective-permute-start | bytes 1253384
  1935.4 372.3 %collective-permute-start.29 = (f32[24,4352]{1,0:T(8,128)S(1)}, f32[24,4352]{1,0:T(8,128)}, u32[]{:S(2)}, u32[]{:S(2)}) collective-permute-start(f32[24,4352]{1,0:T(8,128)S(1)} %get-tuple-element.1751), channel_id=1, source_target_pairs={{0,7},{1,8},{2,9},{3,10},{4,11},{5,12},{6,13},{7,14},{8,15},{9,16}... | collective-permute-start | bytes 1253384
  1937.4 372.3 %collective-permute-start.30 = (f32[24,4352]{1,0:T(8,128)S(1)}, f32[24,4352]{1,0:T(8,128)}, u32[]{:S(2)}, u32[]{:S(2)}) collective-permute-start(f32[24,4352]{1,0:T(8,128)S(1)} %get-tuple-element.1751), channel_id=1, source_target_pairs={{0,8},{1,9},{2,10},{3,11},{4,12},{5,13},{6,14},{7,15},{8,16},{9,17... | collective-permute-start | bytes 1253384
  2301.5 73.7 %collective-permute-start.31 = (f32[24,4352]{1,0:T(8,128)S(1)}, f32[24,4352]{1,0:T(8,128)}, u32[]{:S(2)}, u32[]{:S(2)}) collective-permute-start(f32[24,4352]{1,0:T(8,128)S(1)} %get-tuple-element.1751), channel_id=1, source_target_pairs={{0,9},{1,10},{2,11},{3,12},{4,13},{5,14},{6,15},{7,16},{8,17},{9,1... | collective-permute-start | bytes 1253384
  2303.5 73.1 %collective-permute-start.32 = (f32[24,4352]{1,0:T(8,128)S(1)}, f32[24,4352]{1,0:T(8,128)}, u32[]{:S(2)}, u32[]{:S(2)}) collective-permute-start(f32[24,4352]{1,0:T(8,128)S(1)} %get-tuple-element.1751), channel_id=1, source_target_pairs={{0,10},{1,11},{2,12},{3,13},{4,14},{5,15},{6,16},{7,17},{8,18},{9,... | collective-permute-start | bytes 1253384
  2305.6 79.7 %collective-permute-start.33 = (f32[24,4352]{1,0:T(8,128)S(1)}, f32[24,4352]{1,0:T(8,128)}, u32[]{:S(2)}, u32[]{:S(2)}) collective-permute-start(f32[24,4352]{1,0:T(8,128)S(1)} %get-tuple-element.1751), channel_id=1, source_target_pairs={{0,11},{1,12},{2,13},{3,14},{4,15},{5,16},{6,17},{7,18},{8,19},{9,... | collective-permute-start | bytes 1253384
  2307.6 81.3 %collective-permute-start.34 = (f32[24,4352]{1,0:T(8,128)S(1)}, f32[24,4352]{1,0:T(8,128)}, u32[]{:S(2)}, u32[]{:S(2)}) collective-permute-start(f32[24,4352]{1,0:T(8,128)S(1)} %get-tuple-element.1751), channel_id=1, source_target_pairs={{0,12},{1,13},{2,14},{3,15},{4,16},{5,17},{6,18},{7,19},{8,20},{9,... | collective-permute-start | bytes 1253384
  2309.7 81.5 %collective-permute-start.35 = (f32[24,4352]{1,0:T(8,128)S(1)}, f32[24,4352]{1,0:T(8,128)}, u32[]{:S(2)}, u32[]{:S(2)}) collective-permute-start(f32[24,4352]{1,0:T(8,128)S(1)} %get-tuple-element.1751), channel_id=1, source_target_pairs={{0,13},{1,14},{2,15},{3,16},{4,17},{5,18},{6,19},{7,20},{8,21},{9,... | collective-permute-start | bytes 1253384
  (227 other events, 7538.5 us)
Sparse Core Ops, SparseCore 0:
  11.5 72.8 all-gather.12
  87.8 97.1 all-gather.10
  188.5 114.7 all-gather.16
  306.6 111.6 all-gather.14
  1709.9 305.6 all-reduce.13
where the time goes:
time: 2500 us; the launch traced here: 2490 us
  blocking collectives  1650 us (66%)
  starting transfers between devices  302 us (12%)
  local copies, waits for them, and re-layouts  292 us (12%)
  matrix products  94.4 us (4%)
  other arithmetic  83.9 us (3%)
  waiting for transfers between devices  49.1 us (2%)
    unnamed x3, blocking collectives  1120 us
    all_gather x1, blocking collectives, body(): lax.all_gather(shards[5], 'dp', axis=0, tiled=True)  344 us
    unnamed x49, starting transfers between devices  289 us
    unnamed x265, local copies, waits for them, and re-layouts  188 us
    all_gather x1, blocking collectives, body(): lax.all_gather(shards[4], 'dp', axis=0, tiled=True)  183 us
    select_n x57, other arithmetic, body(): jnp.where(active_step, lax.dynamic_update_index_in_dim(whole, piece, slot...  53.8 us
  transfers between devices with their start and end apart: 57, of which 4 were waited for; matrix products, arithmetic and copies ran while one was open for 21% of the time, Pallas kernels for 0%

commit v1 on v0

v1 whole, which is shorter than its diff:
```python
import jax
import jax.numpy as jnp
from jax import lax
from jax.sharding import Mesh, PartitionSpec as P

HEADS = 17
HDIM = 64
D = HEADS * HDIM
FF = 4 * D
SHARD = 17
NDP = 64
MAIN = 16 * NDP
PAD = 1152
QPAD = 3328

NORM_EPSILON = 1e-05
SCORE_SCALE = 0.125
BF = jnp.bfloat16
F32 = jnp.float32

UP0 = 0
DOWN0 = FF
QKV0 = DOWN0 + 4 * PAD
OUT0 = QKV0 + QPAD
TAIL0 = OUT0 + PAD
TAILW = 896
WIDTH = TAIL0 + TAILW


def matmul(a, b):
    return jnp.dot(a, b, preferred_element_type=F32)


def dot_t(a, b):
    return lax.dot_general(a, b, (((1,), (1,)), ((), ())), preferred_element_type=F32)


def t_dot(a, b):
    return lax.dot_general(a, b, (((0,), (0,)), ((), ())), preferred_element_type=F32)


def order_matrix():
    nat = lax.broadcasted_iota(jnp.int32, (D, D), 0)
    new = lax.broadcasted_iota(jnp.int32, (D, D), 1)
    source = jnp.where(new < MAIN, (new // 16) * SHARD + new % 16, (new - MAIN) * SHARD + 16)
    return (nat == source).astype(BF)


def rows_to_order(rows):
    return jnp.concatenate([rows[:, :16].reshape(MAIN, -1), rows[:, 16]], axis=0)


def hidden_to_order(cols):
    k = cols.shape[0]
    c = cols.reshape(k, NDP, 4, SHARD).transpose(0, 2, 1, 3)
    return jnp.concatenate([c[..., :16].reshape(k, 4, MAIN), c[..., 16]], axis=2).reshape(k, FF)


def hidden_to_natural(cols):
    k = cols.shape[0]
    c = cols.reshape(k, 4, D)
    main = c[..., :MAIN].reshape(k, 4, NDP, 16)
    return jnp.concatenate([main, c[..., MAIN:, None]], axis=3).transpose(0, 2, 1, 3).reshape(k, FF)


def gelu_tanh(v):
    return jax.nn.gelu(v, approximate=True)


def norm_parts(features):
    centred = features - jnp.mean(features, axis=-1, keepdims=True)
    inverse = lax.rsqrt(jnp.mean(centred * centred, axis=-1, keepdims=True) + NORM_EPSILON)
    return centred * inverse, inverse


def norm_back(gradient, normed, inverse, gain):
    gain_grad = jnp.sum(gradient * normed, axis=0)
    bias_grad = jnp.sum(gradient, axis=0)
    scaled = gradient * gain
    centred = scaled - jnp.mean(scaled, axis=-1, keepdims=True)
    centred = centred - normed * jnp.mean(scaled * normed, axis=-1, keepdims=True)
    return inverse * centred, gain_grad, bias_grad


def mm(x, w):
    return matmul(x[:, :MAIN], w[0]) + matmul(x[:, MAIN:], w[1])


def mm_t(g, w):
    return jnp.concatenate([dot_t(g, w[0]), dot_t(g, w[1])], axis=1)


def heads_of(rows):
    return rows.reshape(rows.shape[0], HEADS, HDIM)


def soft_weights_of(q, k, allowed):
    scores = jnp.einsum("qhd,khd->hqk", q, k, preferred_element_type=F32) * SCORE_SCALE
    scores = jnp.where(allowed[None], scores, -1e30)
    e = jnp.exp(scores - jnp.max(scores, axis=-1, keepdims=True))
    return e / jnp.sum(e, axis=-1, keepdims=True)


def forward(x, allowed, order, w, vecs, bias, up_bias):
    normed1, inv1 = norm_parts(x)
    entry = (normed1 * vecs[0] + vecs[1]).astype(BF)
    packed = (mm(entry, w["qkv"]) + bias).astype(BF)
    q, k, v = (heads_of(packed[:, i * D : (i + 1) * D]) for i in range(3))
    soft = soft_weights_of(q, k, allowed)
    mixed = jnp.einsum("hqk,khd->qhd", soft.astype(BF), v, preferred_element_type=F32)
    mixed = matmul(mixed.reshape(-1, D).astype(BF), order).astype(BF)
    middle = x + mm(mixed, w["out"]) + vecs[4]
    normed2, inv2 = norm_parts(middle)
    second = (normed2 * vecs[5] + vecs[6]).astype(BF)
    hidden = mm(second, w["up"]) + up_bias
    active = gelu_tanh(hidden).astype(BF)
    branch = sum(mm(active[:, a * D : (a + 1) * D], w["down"][a]) for a in range(4))
    result = (middle + branch + vecs[7]).astype(BF)
    return result, (normed1, inv1, entry, packed, mixed, normed2, inv2, second, hidden, active)


def backward(grad, allowed, order, w, vecs, kept):
    normed1, inv1, entry, packed, mixed, normed2, inv2, second, hidden, active = kept
    dres = grad.astype(F32)
    dactive = jnp.concatenate([mm_t(grad, w["down"][a]) for a in range(4)], axis=1)
    dhidden = jax.vjp(gelu_tanh, hidden)[1](dactive)[0].astype(BF)
    dsecond = mm_t(dhidden, w["up"])
    dnorm2, dgain2, dbias2 = norm_back(dsecond, normed2, inv2, vecs[5])
    dmiddle = dres + dnorm2
    dattn = dmiddle.astype(BF)
    dmixed = dot_t(mm_t(dattn, w["out"]).astype(BF), order).astype(BF)
    q, k, v = (heads_of(packed[:, i * D : (i + 1) * D]) for i in range(3))
    soft = soft_weights_of(q, k, allowed)
    dm = heads_of(dmixed)
    dsoft = jnp.einsum("qhd,khd->hqk", dm, v, preferred_element_type=F32)
    dscores = (soft * (dsoft - jnp.sum(dsoft * soft, axis=-1, keepdims=True))).astype(BF)
    dv = jnp.einsum("hqk,qhd->khd", soft.astype(BF), dm, preferred_element_type=F32)
    dq = jnp.einsum("hqk,khd->qhd", dscores, k, preferred_element_type=F32) * SCORE_SCALE
    dk = jnp.einsum("hqk,qhd->khd", dscores, q, preferred_element_type=F32) * SCORE_SCALE
    dpacked = jnp.concatenate([p.reshape(-1, D).astype(BF) for p in (dq, dk, dv)], axis=1)
    dentry = mm_t(dpacked, w["qkv"])
    dnorm1, dgain1, dbias1 = norm_back(dentry, normed1, inv1, vecs[0])
    dx = (dmiddle + dnorm1).astype(BF)

    def total(v):
        return jnp.sum(v.astype(F32), axis=0)

    dbias_qv = jnp.stack([total(dpacked[:, :D]), total(dpacked[:, 2 * D :])]).astype(BF)
    dbias_qv = matmul(dbias_qv, order)
    small = jnp.concatenate(
        [
            jnp.stack([dgain1, dbias1]),
            dbias_qv,
            jnp.stack([total(dattn), dgain2, dbias2, total(grad)]),
            total(dhidden).reshape(4, D),
        ],
        axis=0,
    )
    return dx, (dhidden, dattn, dpacked, grad, small)


def pad_cols(v, width):
    return jnp.pad(v, ((0, 0), (0, width - v.shape[1])))


def body(inputs, cotangent, lengths, vectors, qkv_w, out_w, up_w, up_b, down_w):
    section = lax.axis_index("section")
    zi = lax.axis_index("z")
    mb, rows, _ = inputs.shape
    n = mb * rows
    order = order_matrix()

    outdown = matmul(jnp.concatenate([out_w[0], down_w[0]], axis=0), order).astype(BF)
    shard = [hidden_to_order(up_w[0])]
    shard += [pad_cols(outdown[SHARD * (1 + a) : SHARD * (2 + a)], PAD) for a in range(4)]
    shard += [pad_cols(qkv_w[0], QPAD), pad_cols(outdown[:SHARD], PAD)]
    shard = jnp.concatenate(shard, axis=1)
    tail = jnp.concatenate([shard[16], vectors[0].reshape(-1), up_b[0]])
    tail = jnp.pad(tail, (0, 16 * TAILW - tail.shape[0])).reshape(16, TAILW)
    sent = jnp.concatenate([shard[:16], tail], axis=1)
    whole = lax.all_gather(sent, ("x", "y", "z"), axis=0, tiled=True)
    tails = whole[:, TAIL0:].reshape(NDP, 16 * TAILW)
    vec_all = tails[:, TAIL0 : TAIL0 + SHARD * 8].reshape(NDP, SHARD, 8).astype(F32)
    upb_all = tails[:, TAIL0 + SHARD * 8 : TAIL0 + SHARD * 12].reshape(NDP, 4, SHARD).astype(F32)

    def weight(start, width):
        return whole[:, start : start + width], tails[:, start : start + width]

    w = {
        "up": weight(UP0, FF),
        "down": [weight(DOWN0 + a * PAD, D) for a in range(4)],
        "qkv": weight(QKV0, 3 * D),
        "out": weight(OUT0, D),
    }
    vecs = rows_to_order(vec_all).T
    vec_nat = vec_all.reshape(D, 8)
    bias = jnp.concatenate([vec_nat[:, 2], jnp.zeros((D,), F32), vec_nat[:, 3]])
    up_bias = rows_to_order(upb_all.transpose(0, 2, 1)).T.reshape(FF)

    ends = jnp.cumsum(lengths[:, 0], axis=1)
    place = jnp.arange(rows, dtype=jnp.int32)
    seg = jnp.sum((place[None, :, None] >= ends[:, None, :]).astype(jnp.int32), axis=2)
    seg = (seg + 8 * jnp.arange(mb, dtype=jnp.int32)[:, None]).reshape(n)
    at = jnp.arange(n, dtype=jnp.int32)
    allowed = (seg[:, None] == seg[None, :]) & (at[:, None] >= at[None, :])

    x0 = matmul(inputs.reshape(n, D), order).astype(BF)
    cot = matmul(cotangent.reshape(n, D), order).astype(BF)

    def fwd(x):
        return forward(x.astype(F32), allowed, order, w, vecs, bias, up_bias)

    def bwd(grad, kept):
        return backward(grad, allowed, order, w, vecs, kept)

    def zeros_like_tree(t):
        return jax.tree.map(lambda s: jnp.zeros(s.shape, s.dtype), t)

    fwd_shape = jax.eval_shape(fwd, x0)
    bwd_shape = jax.eval_shape(bwd, cot, fwd_shape[1])
    first = lax.cond(section == 0, fwd, lambda x: zeros_like_tree(fwd_shape), x0)
    arrived = lax.ppermute(first[0], "section", [(0, 1)])

    def top(x, first):
        res, kept = fwd(x)
        dx, factors = bwd(cot, kept)
        return res, kept, dx, factors

    def keep(x, first):
        return first[0], first[1], *zeros_like_tree(bwd_shape)

    result, kept, dx, factors = lax.cond(section == 1, top, keep, arrived, first)
    coming = lax.ppermute(dx, "section", [(1, 0)])
    dx, factors = lax.cond(
        section == 0,
        lambda g, old: bwd(g, kept),
        lambda g, old: old,
        coming,
        (dx, factors),
    )

    entry, mixed, second, active = kept[2], kept[4], kept[7], kept[9]
    dhidden, dattn, dpacked, dbranch, small = factors
    blocks = jnp.stack(
        [
            jnp.stack([entry, entry, entry, mixed]),
            jnp.stack([dpacked[:, :D], dpacked[:, D : 2 * D], dpacked[:, 2 * D :], dattn]),
            active.reshape(n, 4, D).transpose(1, 0, 2),
            dhidden.reshape(n, 4, D).transpose(1, 0, 2),
        ]
    )

    def for_z(target):
        own = lax.dynamic_index_in_dim(blocks, target, 1, keepdims=False)
        return jnp.concatenate([own, second[None], dbranch[None]], axis=0)

    parts = [for_z(zi)]
    for d in (1, 2, 3):
        parts.append(
            lax.ppermute(for_z((zi + d) % 4), "z", [(i, (i + d) % 4) for i in range(4)])
        )
    a_attn, b_attn, act_z, dhid_z, sec_all, db_all = jnp.concatenate(parts, axis=1)
    pairs = ((sec_all, dhid_z), (act_z, db_all), (a_attn, b_attn))

    main = jnp.concatenate([t_dot(a[:, :MAIN], b).astype(BF) for a, b in pairs], axis=1)
    last = jnp.concatenate([t_dot(a[:, MAIN:], b).astype(BF) for a, b in pairs], axis=1)
    small_t = pad_cols(small.T.astype(BF), QPAD - 3 * D)
    main = jnp.concatenate([main, small_t[:MAIN]], axis=1).reshape(16, 64, QPAD)
    last = jnp.concatenate([last, small_t[MAIN:]], axis=1).reshape(16, 4, QPAD)
    payload = jnp.concatenate([main, last, jnp.zeros((16, 4, QPAD), BF)], axis=1)
    got = lax.psum_scatter(
        payload.reshape(16 * 72, QPAD), ("x", "y"), scatter_dimension=0, tiled=True
    )
    to_z = jnp.concatenate(
        [got[:64].reshape(4, 16, QPAD), got[64:68].reshape(4, 1, QPAD), jnp.zeros((4, 7, QPAD), BF)],
        axis=1,
    )
    mine = lax.all_to_all(to_z, "z", 0, 0, tiled=True)[:, :SHARD]

    g_up = hidden_to_natural(mine[:, :, :D].transpose(1, 0, 2).reshape(SHARD, FF)).astype(F32)
    cols = jnp.concatenate(
        [mine[:, :, D : 2 * D].reshape(4 * SHARD, D), mine[3, :, 2 * D : 3 * D]], axis=0
    )
    cols = dot_t(cols, order)
    g_qkv = mine[:3, :, 2 * D : 3 * D].transpose(1, 0, 2).reshape(SHARD, 3 * D).astype(F32)
    sums = jnp.sum(mine[:, :, 3 * D : 3 * D + 12].astype(F32), axis=0)
    back = dot_t(jnp.concatenate([result, dx], axis=0), order).astype(BF)
    acts = back[:n].reshape(1, mb, rows, D)
    grads = back[n:].reshape(1, mb, rows, D)
    return (
        acts,
        grads,
        sums[None, :, :8],
        g_qkv[None],
        cols[None, 4 * SHARD :],
        g_up[None],
        sums[:, 8:].T.reshape(1, 4 * SHARD),
        cols[None, : 4 * SHARD],
    )


def solution(mesh):
    grid = Mesh(mesh.devices.reshape(2, 4, 4, 4), ("section", "x", "y", "z"))
    dp = ("x", "y", "z")
    tokens = P(None, dp, None)
    rows = P("section", dp, None)
    in_specs = (tokens, tokens, tokens, rows, rows, rows, rows, P("section", dp), rows)
    stacked = P("section", None, dp, None)
    out_specs = (stacked, stacked, rows, rows, rows, rows, P("section", dp), rows)
    return jax.shard_map(body, mesh=grid, in_specs=in_specs, out_specs=out_specs, check_vma=False)
```

time: 2500 us -> 732 us (0.29)
  blocking collectives: 1650 us -> 0 us
  waiting for transfers between devices: 49.1 us -> 428 us
  starting transfers between devices: 302 us -> 13.6 us
  local copies, waits for them, and re-layouts: 292 us -> 119 us
  other arithmetic: 83.9 us -> 47.7 us
    unnamed x3 -> x0, blocking collectives: 1120 us -> none
    all_gather x2 -> x0, blocking collectives: 527 us -> none  [the longest x1 344 us: body(): lax.all_gather(shards[5], 'dp', axis=0, tiled=True)]
    unnamed x49 -> x1, starting transfers between devices: 289 us -> 0.57 us
    unnamed x265 -> x61, local copies, waits for them, and re-layouts: 188 us -> 7.47 us
    all_gather x4 -> x1, waiting for transfers between devices: 0.03 us -> 144 us  [body(): whole = lax.all_gather(sent, ('x', 'y', 'z'), axis=0, tiled=True)]
    unnamed x54 -> x3, waiting for transfers between devices: 11.7 us -> 130 us
    ppermute x4 -> x5, waiting for transfers between devices: 37.4 us -> 144 us  [the longest x1 109 us: body(): coming = lax.ppermute(dx, 'section', [(1, 0)])]
    select_n x63 -> x0, other arithmetic: 57.7 us -> none  [the longest x57 53.8 us: body(): jnp.where(active_step, lax.dynamic_update_index_in_dim(whole, piece, slot...]
  transfers between devices with their start and end apart: 57 -> 8, of which waited for: 4 -> 7; matrix products, arithmetic and copies ran while one was open for 21% -> 3% of each run, Pallas kernels for 0% -> 0%
where the time goes in v1:
time: 732 us; the launch traced here: 728 us
  waiting for transfers between devices  428 us (58%)
  local copies, waits for them, and re-layouts  119 us (16%)
  matrix products  99.3 us (14%)
  other arithmetic  47.7 us (7%)
  between operations  15.6 us (2%)
  starting transfers between devices  13.6 us (2%)
    all_gather x1, waiting for transfers between devices, body(): whole = lax.all_gather(sent, ('x', 'y', 'z'), axis=0, tiled=True)  144 us
    unnamed x3, waiting for transfers between devices  130 us
    ppermute x1, waiting for transfers between devices, body(): coming = lax.ppermute(dx, 'section', [(1, 0)])  109 us
    dot_general x19, matrix products, matmul(): return jnp.dot(a, b, preferred_element_type=F32)  44.5 us
    dot_general x17, matrix products, dot_t(): lax.dot_general(a, b, (((1,), (1,)), ((), ())), preferred_element_type=F32)  35.7 us
    ppermute x3, waiting for transfers between devices, body(): lax.ppermute(for_z((zi + d) % 4), 'z', [(i, (i + d) % 4) for i in range(4)])  35.1 us
    slice x6, local copies, waits for them, and re-layouts, weight(): return (whole[:, start:start + width], tails[:, start:start + width])  28.4 us
  transfers between devices with their start and end apart: 8, of which 7 were waited for; matrix products, arithmetic and copies ran while one was open for 3% of the time, Pallas kernels for 0%

profile of v1, /device:TPU:0, one launch (start us, length us, event | category | flops | bytes accessed | tf_op | source)
XLA Modules:
  0.0 728.1 jit_solution(8639765153990907919)
XLA Ops:
  30.4 144.5 %all-gather.2.cloned.1.call-done = bf16[1024,14336]{1,0:T(8,128)(2,1)} async-done(((bf16[16,14336]{1,0:T(8,128)(2,1)}), bf16[1024,14336]{1,0:T(8,128)(2,1)}) %all-gather.2.cloned.1.call-update) | async-done | bytes 29360144 | tf_op jit(solution)/shard_map/all_gather | solution.py:181
  177.8 3.8 reshape.396
  194.2 8.7 %fusion.201 = (bf16[1024,1088]{1,0:T(8,128)(2,1)}, bf16[1024,1088]{1,0:T(8,128)(2,1)}, bf16[1024,1088]{1,0:T(8,128)(2,1)}, bf16[1024,1088]{1,0:T(8,128)(2,1)}, bf16[1024,1088]{1,0:T(8,128)(2,1)}) fusion(bf16[1024,14336]{1,0:T(8,128)(2,1)} %all-gather.2.cloned.1.call-done), kind=kLoop, calls=%fused_computation.392 | loop fusion | bytes 22282240 | tf_op jit(solution)/shard_map/slice | solution.py:187
  202.8 7.7 %slice.487 = bf16[1024,4352]{1,0:T(8,128)(2,1)} slice(bf16[1024,14336]{1,0:T(8,128)(2,1)} %all-gather.2.cloned.1.call-done), slice={[0:1024], [0:4352]} | slice | bytes 17825792 | tf_op jit(solution)/shard_map/slice | solution.py:187
  210.5 6.3 slice.481
  216.8 50.4 %conditional.3 = (bf16[128,1088]{0,1:T(8,128)(2,1)}, f32[128,1088]{0,1:T(8,128)}, f32[128,1]{0,1:T(1,128)}, bf16[128,1088]{0,1:T(8,128)(2,1)}, bf16[128,3264]{0,...) conditional(s32[]{:T(128)} %convert_element_type.380, () %tuple.44, ...), branch_computations={%region_2.3_spmd, %region_3.10_spmd} | conditional | flops 4061497856 | bytes 116874032 | solution.py:221
  219.7 5.8 fusion.38
  241.4 6.4 fusion.34
  247.9 4.8 fusion.19
  271.5 7.7 %conditional.4 = (bf16[128,1088]{0,1:T(8,128)(2,1)}, f32[128,1088]{0,1:T(8,128)}, f32[128,1]{0,1:T(1,128)}, bf16[128,1088]{0,1:T(8,128)(2,1)}, bf16[128,3264]{0,...) conditional(s32[]{:T(128)} %convert_element_type.379, ...), branch_computations={%region_10.11_spmd, %region_11.32_spmd} | conditional | flops 8206129152 | bytes 279785408 | solution.py:232
  287.3 109.3 %collective-permute-done.1 = bf16[128,1088]{1,0:T(8,128)(2,1)S(1)} collective-permute-done((bf16[128,1088]{1,0:T(8,128)(2,1)}, bf16[128,1088]{1,0:T(8,128)(2,1)S(1)}, u32[]{:S(2)}, u32[]{:S(2)}) %collective-permute-start.1) | collective-permute-done | bytes 278560 | tf_op jit(solution)/shard_map/ppermute | solution.py:233
  396.6 71.9 %conditional.5 = (bf16[128,1088]{1,0:T(8,128)(2,1)}, bf16[128,4352]{1,0:T(8,128)(2,1)}, bf16[12,1088]{1,0:T(8,128)(2,1)}, bf16[1,128,1088]{1,2,0:T(8,128)(2,1)},...) conditional(s32[]{:T(128)} %convert_element_type.380, ...), branch_computations={%region_32.33_spmd, %region_33.50_spmd} | conditional | flops 4186689024 | bytes 131772216 | solution.py:234
  408.2 4.7 concatenate.78
  412.9 5.5 convert_reduce_fusion.5
  418.4 7.7 %fusion.225 = f32[128,1024]{1,0:T(8,128)} fusion(bf16[128,4352]{1,0:T(8,128)(2,1)} %get-tuple-element.899, bf16[1024,4352]{1,0:T(8,128)(2,1)} %get-tuple-element.306), kind=kOutput, calls=%fused_computation.416 | convolution fusion | flops 1140850688 | bytes 10551296 | tf_op jit(solution)/shard_map/cond/branch_1_fun/dot_general | solution.py:35
  455.6 5.6 fusion.134
  486.4 16.3 %collective-permute-done.2 = bf16[6,128,1088]{1,2,0:T(8,128)(2,1)} collective-permute-done((bf16[6,128,1088]{1,2,0:T(8,128)(2,1)}, bf16[6,128,1088]{1,2,0:T(8,128)(2,1)}, u32[]{:S(2)}, u32[]{:S(2)}) %collective-permute-start.2) | collective-permute-done | bytes 1671200 | tf_op jit(solution)/shard_map/ppermute | solution.py:260
  502.7 18.4 %collective-permute-done.3 = bf16[6,128,1088]{1,2,0:T(8,128)(2,1)} collective-permute-done((bf16[6,128,1088]{1,2,0:T(8,128)(2,1)}, bf16[6,128,1088]{1,2,0:T(8,128)(2,1)}, u32[]{:S(2)}, u32[]{:S(2)}) %collective-permute-start.3) | collective-permute-done | bytes 1671200 | tf_op jit(solution)/shard_map/ppermute | solution.py:260
  530.6 3.7 pad_maximum_fusion.8
  534.3 9.6 %copy.419 = bf16[1024,3328]{1,0:T(8,128)(2,1)} copy(bf16[1024,3328]{0,1:T(8,128)(2,1)} %pad_maximum_fusion.8) | data formatting | bytes 13631488 | tf_op jit(solution)/shard_map/concatenate | solution.py:268
  544.2 7.5 %maximum_maximum_fusion = bf16[16,72,3328]{2,1,0:T(8,128)(2,1)} fusion(bf16[16,4,3328]{2,1,0:T(4,128)(2,1)S(1)} %reshape.405, bf16[16,64,3328]{2,1,0:T(8,128)(2,1)} %bitcast.294, bf16[72]{0:T(256)(128)(2,1)S(1)} %pad.67.clone), kind=kLoop, calls=%fused_computation.270 | loop fusion | flops 23003136 | bytes 14909584 | tf_op jit(solution)/shard_map/concatenate | solution.py:270
  556.7 130.1 %all-reduce.11.cloned.1.call-done = bf16[1152,3328]{1,0:T(8,128)(2,1)} async-done(((bf16[1152,3328]{1,0:T(8,128)(2,1)}), bf16[1152,3328]{1,0:T(8,128)(2,1)}) %all-reduce.11.cloned.1.call-update) | async-done | bytes 7667728
  689.8 4.6 all-to-all-start
  696.3 8.8 %all-to-all-done = bf16[4,24,3328]{2,1,0:T(8,128)(2,1)S(1)} async-done(((bf16[4,24,3328]{2,1,0:T(8,128)(2,1)}), bf16[4,24,3328]{2,1,0:T(8,128)(2,1)S(1)}, u32[]{:S(2)}, u32[]{:S(2)}) %all-to-all-start) | async-done | bytes 639008 | tf_op jit(solution)/shard_map/all_to_all | solution.py:278
  (342 shorter events, 187.9 us)
Async XLA Ops:
  7.2 20.4 %copy-start = (bf16[2,64,1088]{2,1,0:T(8,128)(2,1)S(1)}, bf16[2,64,1088]{2,1,0:T(8,128)(2,1)}, u32[]{:S(2)}) copy-start(bf16[2,64,1088]{2,1,0:T(8,128)(2,1)} %param.15) | copy-start | bytes 835588
  7.2 167.7 %all-gather.2.cloned.1.call-start = ((), (), s32[]{:S(2)}) async-start(), calls=%async_computation.1 | async-start | bytes 29818880 | tf_op jit(solution)/shard_map/all_gather | solution.py:181
  25.8 661.0 %all-reduce.11.cloned.1.call-start = ((), (), s32[]{:S(2)}) async-start(), calls=%async_computation.2 | async-start | bytes 15335424
  186.3 85.2 %copy-start.47 = (bf16[64,1088]{1,0:T(8,128)(2,1)}, bf16[64,1088]{1,0:T(8,128)(2,1)S(1)}, u32[]{:S(2)}) copy-start(bf16[64,1088]{1,0:T(8,128)(2,1)S(1)} %get-tuple-element.811) | copy-start | bytes 417796
  193.5 78.1 %copy-start.76 = (f32[8,1088]{1,0:T(8,128)}, f32[8,1088]{1,0:T(8,128)S(1)}, u32[]{:S(2)}) copy-start(f32[8,1088]{1,0:T(8,128)S(1)} %maximum_bitcast_fusion.2) | copy-start | bytes 104452
  194.2 22.6 %copy-start.84 = (f32[3264]{0:T(1024)}, f32[3264]{0:T(1024)S(1)}, u32[]{:S(2)}) copy-start(f32[3264]{0:T(1024)S(1)} %concatenate.110) | copy-start | bytes 39172
  210.5 6.3 copy-start.31
  210.5 6.3 copy-start.46
  210.5 6.3 copy-start.87
  217.0 12.9 %copy-start.88 = (pred[128,128]{0,1:T(8,128)(4,1)}, pred[128,128]{0,1:T(8,128)(4,1)S(1)}, u32[]{:S(2)}) copy-start(pred[128,128]{0,1:T(8,128)(4,1)S(1)} %get-tuple-element.240) | copy-start | bytes 49156 | tf_op jit(solution)/shard_map/cond
  241.4 6.4 copy-start.82
  247.9 4.8 copy-start.10
  267.2 4.3 collective-permute-start
  281.1 115.5 %collective-permute-start.1 = (bf16[128,1088]{1,0:T(8,128)(2,1)}, bf16[128,1088]{1,0:T(8,128)(2,1)S(1)}, u32[]{:S(2)}, u32[]{:S(2)}) collective-permute-start(bf16[128,1088]{1,0:T(8,128)(2,1)} %copy.403), channel_id=1, source_target_pairs={{64,0},{65,1},{66,2},{67,3},{68,4},{69,5},{70,6},{71,7},{72,8},{73... | collective-permute-start | bytes 835592 | tf_op jit(solution)/shard_map/ppermute | solution.py:233
  282.4 114.2 %copy-start.33 = (bf16[64,3264]{1,0:T(8,128)(2,1)S(1)}, bf16[64,3264]{1,0:T(8,128)(2,1)}, u32[]{:S(2)}) copy-start(bf16[64,3264]{1,0:T(8,128)(2,1)} %slice.482) | copy-start | bytes 1253380
  418.4 7.7 %copy-start.41 = (bf16[64,4352]{1,0:T(8,128)(2,1)S(1)}, bf16[64,4352]{1,0:T(8,128)(2,1)}, u32[]{:S(2)}) copy-start(bf16[64,4352]{1,0:T(8,128)(2,1)} %get-tuple-element.307) | copy-start | bytes 1671172 | tf_op jit(solution)/shard_map/cond
  427.7 5.8 copy-start.75
  431.3 5.2 copy-start.19
  439.8 4.5 copy-start.90
  479.7 23.0 %collective-permute-start.2 = (bf16[6,128,1088]{1,2,0:T(8,128)(2,1)}, bf16[6,128,1088]{1,2,0:T(8,128)(2,1)}, u32[]{:S(2)}, u32[]{:S(2)}) collective-permute-start(bf16[6,128,1088]{1,2,0:T(8,128)(2,1)} %get-tuple-element.818), channel_id=1, source_target_pairs={{0,1},{1,2},{2,3},{3,0},{4,5},{5,6},{6,7},{7,4},{8,9},{9,10},{10,1... | collective-permute-start | bytes 5013512 | tf_op jit(solution)/shard_map/ppermute | solution.py:260
  480.5 40.5 %collective-permute-start.3 = (bf16[6,128,1088]{1,2,0:T(8,128)(2,1)}, bf16[6,128,1088]{1,2,0:T(8,128)(2,1)}, u32[]{:S(2)}, u32[]{:S(2)}) collective-permute-start(bf16[6,128,1088]{1,2,0:T(8,128)(2,1)} %get-tuple-element.819), channel_id=1, source_target_pairs={{0,2},{1,3},{2,0},{3,1},{4,6},{5,7},{6,4},{7,5},{8,10},{9,11},{10,... | collective-permute-start | bytes 5013512 | tf_op jit(solution)/shard_map/ppermute | solution.py:260
  483.4 38.1 %collective-permute-start.4 = (bf16[6,128,1088]{1,2,0:T(8,128)(2,1)}, bf16[6,128,1088]{1,2,0:T(8,128)(2,1)}, u32[]{:S(2)}, u32[]{:S(2)}) collective-permute-start(bf16[6,128,1088]{1,2,0:T(8,128)(2,1)} %get-tuple-element.820), channel_id=1, source_target_pairs={{0,3},{1,0},{2,1},{3,2},{4,7},{5,4},{6,5},{7,6},{8,11},{9,8},{10,9... | collective-permute-start | bytes 5013512 | tf_op jit(solution)/shard_map/ppermute | solution.py:260
  689.8 15.3 %all-to-all-start = ((bf16[4,24,3328]{2,1,0:T(8,128)(2,1)}), bf16[4,24,3328]{2,1,0:T(8,128)(2,1)S(1)}, u32[]{:S(2)}, u32[]{:S(2)}) async-start(bf16[4,24,3328]{2,1,0:T(8,128)(2,1)} %maximum_maximum_fusion.1), calls=%async_computation | async-start | bytes 1277952 | tf_op jit(solution)/shard_map/all_to_all | solution.py:278
  712.4 8.6 %copy-start.1 = (bf16[2,64,1088]{2,1,0:T(8,128)(2,1)S(1)}, bf16[2,64,1088]{2,1,0:T(8,128)(2,1)}, u32[]{:S(2)}) copy-start(bf16[2,64,1088]{2,1,0:T(8,128)(2,1)} %param.15) | copy-start | bytes 835588
  (50 other events, 111.3 us)
Sparse Core Ops, SparseCore 0:
  26.0 148.8 all-gather.1
  551.9 134.8 all-reduce.10

commit v2 on v1

v2 whole, which is shorter than its diff:
```python
import functools

import jax
import jax.numpy as jnp
import numpy as np
from jax import lax
from jax.experimental import pallas as pl
from jax.experimental.pallas import tpu as pltpu
from jax.sharding import Mesh, PartitionSpec as P

HEADS = 17
HDIM = 64
D = HEADS * HDIM
FF = 4 * D
SHARD = 17
NDP = 64
MAIN = 16 * NDP
PAD = 1152
ROWS = 128
PAIRS = PAD // 128

UP, DOWN, QKV, OUT, BLOCKS = 0, 4, 8, 11, 12
TAIL0 = BLOCKS * PAD
TAILW = 896
WIDTH = TAIL0 + TAILW
SMALLS = 256

NORM_EPSILON = 1e-05
SCORE_SCALE = 0.125
GELU_C = float(np.sqrt(2 / np.pi))
GELU_A = 0.044715
BF = jnp.bfloat16
F32 = jnp.float32
VMEM_BYTES = 58 * 1024 * 1024


def constants():
    n = np.arange(D)
    shard_of = np.where(n < MAIN, n // 16, n - MAIN)
    row_of = np.where(n < MAIN, n % 16, 16)
    order = np.zeros((PAD, D), np.float32)
    order[shard_of * SHARD + row_of, n] = 1
    f = np.arange(D)
    s, a, r = f // 68, (f % 68) // SHARD, f % SHARD
    hid = np.zeros((D, D), np.float32)
    hid[f, np.where(r < 16, a * 256 + s * 16 + r, 1024 + a * 16 + s)] = 1
    k = np.arange(SMALLS)
    is_vec, is_up = k < 136, (k >= 136) & (k < 204)
    k_row = np.where(is_vec, k // 8, np.where(is_up, (k - 136) % SHARD, -1))
    k_out = np.where(is_vec, k % 8, np.where(is_up, 8 + (k - 136) // SHARD, -1))
    pick = (k_out[None, :] == np.arange(16)[:, None]).astype(np.float32)
    spread = (np.arange(NDP)[:, None] == shard_of[None, :]).astype(np.float32)
    keep = (k_row[:, None] == row_of[None, :]).astype(np.float32)
    nat = np.arange(PAD)
    spread_nat = (np.arange(NDP)[:, None] == nat[None, :] // SHARD).astype(np.float32)
    keep_nat = (k_row[:, None] == nat[None, :] % SHARD).astype(np.float32)
    m = np.arange(MAIN)
    turn = np.zeros((MAIN, MAIN), np.float32)
    turn[(m % 16) * NDP + m // 16, m] = 1
    names = ("order", "hid", "pick", "spread", "keep", "spread_nat", "keep_nat", "turn")
    values = (order, hid, pick, spread, keep, spread_nat, keep_nat, turn)
    return {name: jnp.asarray(value, BF) for name, value in zip(names, values)}


def matmul(a, b):
    return jnp.dot(a, b, preferred_element_type=F32)


def dot_t(a, b):
    return lax.dot_general(a, b, (((1,), (1,)), ((), ())), preferred_element_type=F32)


def t_dot(a, b):
    return lax.dot_general(a, b, (((0,), (0,)), ((), ())), preferred_element_type=F32)


def norm_parts(features):
    centred = features - jnp.mean(features, axis=-1, keepdims=True)
    inverse = lax.rsqrt(jnp.mean(centred * centred, axis=-1, keepdims=True) + NORM_EPSILON)
    return centred * inverse, inverse


def norm_back(gradient, normed, inverse, gain):
    scaled = gradient * gain
    centred = scaled - jnp.mean(scaled, axis=-1, keepdims=True)
    return inverse * (centred - normed * jnp.mean(scaled * normed, axis=-1, keepdims=True))


def col_sum(v):
    return jnp.sum(v, axis=0, keepdims=True)


def unpack_kernel(whole, pick, spread, keep, spread_nat, keep_nat, turn, tails, vecs, nat, raw, sem):
    copy = pltpu.make_async_copy(whole.at[:, pl.ds(TAIL0, TAILW)], raw, sem)
    copy.start()
    copy.wait()
    turned = matmul(turn[...], raw[...]).astype(BF)
    for j in range(16):
        tails[:, j * TAILW : (j + 1) * TAILW] = turned[j * NDP : (j + 1) * NDP]
    small = tails[:, TAIL0 : TAIL0 + SMALLS]
    for out, s, k in ((vecs, spread, keep), (nat, spread_nat, keep_nat)):
        wide = t_dot(small, s[...]) * k[...].astype(F32)
        out[...] = matmul(pick[...], wide.astype(BF))


def unpack(whole, c):
    vm = pl.BlockSpec(memory_space=pltpu.VMEM)
    return pl.pallas_call(
        unpack_kernel,
        in_specs=[pl.BlockSpec(memory_space=pl.ANY)] + [vm] * 6,
        out_specs=[vm] * 3,
        out_shape=[
            jax.ShapeDtypeStruct((NDP, 16 * TAILW), BF),
            jax.ShapeDtypeStruct((16, D), F32),
            jax.ShapeDtypeStruct((16, PAD), F32),
        ],
        scratch_shapes=[pltpu.VMEM((MAIN, TAILW), BF), pltpu.SemaphoreType.DMA],
        compiler_params=pltpu.CompilerParams(vmem_limit_bytes=VMEM_BYTES),
        name="unpack",
    )(whole, c["pick"], c["spread"], c["keep"], c["spread_nat"], c["keep_nat"], c["turn"])


class Weights:
    def __init__(self, whole, tails, buf, sems):
        self.whole, self.tails, self.buf, self.sems = whole, tails, buf, sems

    def copies(self, b):
        cols = pl.ds(b * PAD, PAD)
        return (
            pltpu.make_async_copy(
                self.whole.at[:, cols], self.buf.at[b, pl.ds(0, MAIN)], self.sems.at[b, 0]
            ),
            pltpu.make_async_copy(
                self.tails.at[:, cols], self.buf.at[b, pl.ds(MAIN, NDP)], self.sems.at[b, 1]
            ),
        )

    def start(self, blocks):
        for b in blocks:
            for copy in self.copies(b):
                copy.start()

    def wait(self, b):
        for copy in self.copies(b):
            copy.wait()


def pair_masks():
    lane = lax.broadcasted_iota(jnp.int32, (ROWS, 128), 1)
    first = (lane < HDIM).astype(F32)
    return first, 1.0 - first


def stacked(v, masks):
    return jnp.concatenate([(v * m).astype(BF) for m in masks], axis=0)


def soft_pair(q, kk, allowed):
    scores = dot_t(q, kk) * SCORE_SCALE
    halves = []
    for h in range(2):
        s = jnp.where(allowed, scores[:, h * ROWS : (h + 1) * ROWS], -1e30)
        e = jnp.exp(s - jnp.max(s, axis=-1, keepdims=True))
        halves.append(e / jnp.sum(e, axis=-1, keepdims=True))
    return halves


def forward_part(w, wait, x_ref, pairs_ref, vecs, nat, order, r):
    x = x_ref[...].astype(F32)
    normed, _ = norm_parts(x)
    r["entry"][...] = (normed * vecs[0:1] + vecs[1:2]).astype(BF)

    def project(i, carry):
        if wait:
            w.wait(QKV + i)
        shift = jnp.where(i == 0, nat[2:3], jnp.where(i == 2, nat[3:4], 0.0))
        r["packed"][i] = (matmul(r["entry"][...], w.buf[QKV + i]) + shift).astype(BF)
        return carry

    lax.fori_loop(0, 3, project, 0)
    masks = pair_masks()
    allowed = pairs_ref[...] > 0
    for p in range(PAIRS):
        cols = pl.ds(p * 128, 128)
        kk = stacked(r["packed"][1, :, cols].astype(F32), masks)
        vv = stacked(r["packed"][2, :, cols].astype(F32), masks)
        halves = soft_pair(r["packed"][0, :, cols], kk, allowed)
        soft = jnp.concatenate([h.astype(BF) for h in halves], axis=1)
        r["heads"][:, cols] = matmul(soft, vv).astype(BF)
    r["mixed"][...] = matmul(r["heads"][...], order[...]).astype(BF)
    if wait:
        w.wait(OUT)
    branch = matmul(r["mixed"][...], w.buf[OUT])[:, :D]
    middle = x + branch + vecs[4:5]
    r["middle"][...] = middle
    normed, _ = norm_parts(middle)
    r["second"][...] = (normed * vecs[5:6] + vecs[6:7]).astype(BF)
    r["acc"][...] = jnp.zeros((ROWS, PAD), F32)

    def feed(a, carry):
        if wait:
            w.wait(UP + a)
        hidden = matmul(r["second"][...], w.buf[UP + a])[:, :D] + vecs[pl.ds(8 + a, 1)]
        r["hidden"][a] = hidden
        bent = jnp.tanh(GELU_C * (hidden + GELU_A * (hidden * hidden * hidden)))
        r["active"][a] = (0.5 * hidden * (1.0 + bent)).astype(BF)
        if wait:
            w.wait(DOWN + a)
        r["acc"][...] += matmul(r["active"][a], w.buf[DOWN + a])
        return carry

    lax.fori_loop(0, 4, feed, 0)
    r["result"][...] = (r["middle"][...] + r["acc"][:, :D] + vecs[7:8]).astype(BF)


def backward_part(w, wait, grad_ref, x_ref, pairs_ref, vecs, order, r):
    grad = grad_ref[...]
    dres = grad.astype(F32)
    r["acc"][...] = jnp.zeros((ROWS, PAD), F32)

    def feed(a, carry):
        if wait:
            w.wait(DOWN + a)
        dactive = dot_t(grad_ref[...], w.buf[DOWN + a, :, :D])
        h = r["hidden"][a]
        square = h * h
        bent = jnp.tanh(GELU_C * (h + GELU_A * (square * h)))
        slope = 0.5 * (1.0 + bent) + (0.5 * GELU_C) * h * (1.0 - bent * bent) * (
            1.0 + (3 * GELU_A) * square
        )
        dhidden = (dactive * slope).astype(BF)
        r["dhidden"][a] = dhidden
        r["small"][pl.ds(8 + a, 1)] = col_sum(dhidden.astype(F32))
        if wait:
            w.wait(UP + a)
        r["acc"][:, :D] += dot_t(dhidden, w.buf[UP + a, :, :D])
        return carry

    lax.fori_loop(0, 4, feed, 0)
    dsecond = r["acc"][:, :D]
    normed, inverse = norm_parts(r["middle"][...])
    r["small"][5:6] = col_sum(dsecond * normed)
    r["small"][6:7] = col_sum(dsecond)
    r["small"][7:8] = col_sum(dres)
    dmiddle = dres + norm_back(dsecond, normed, inverse, vecs[5:6])
    r["middle"][...] = dmiddle
    dattn = dmiddle.astype(BF)
    r["dpacked"][3] = dattn
    r["small"][4:5] = col_sum(dattn.astype(F32))
    if wait:
        w.wait(OUT)
    dmixed = dot_t(dattn, w.buf[OUT, :, :D]).astype(BF)
    r["heads"][...] = dot_t(dmixed, order[...]).astype(BF)
    masks = pair_masks()
    allowed = pairs_ref[...] > 0
    for p in range(PAIRS):
        cols = pl.ds(p * 128, 128)
        width = min(D - p * 128, 128)
        live = pl.ds(p * 128, width)
        q = r["packed"][0, :, cols]
        kk = stacked(r["packed"][1, :, cols].astype(F32), masks)
        vv = stacked(r["packed"][2, :, cols].astype(F32), masks)
        dm = r["heads"][:, cols]
        halves = soft_pair(q, kk, allowed)
        dsoft = dot_t(dm, vv)
        dscores = []
        for h, p_half in enumerate(halves):
            d_half = dsoft[:, h * ROWS : (h + 1) * ROWS]
            centre = jnp.sum(d_half * p_half, axis=-1, keepdims=True)
            dscores.append((p_half * (d_half - centre)).astype(BF))
        ds = jnp.concatenate(dscores, axis=1)
        soft = jnp.concatenate([h.astype(BF) for h in halves], axis=1)
        dq = matmul(ds, kk) * SCORE_SCALE
        dk = t_dot(ds, q) * SCORE_SCALE
        dv = t_dot(soft, dm)
        dk = dk[:ROWS] * masks[0] + dk[ROWS:] * masks[1]
        dv = dv[:ROWS] * masks[0] + dv[ROWS:] * masks[1]
        for i, v in enumerate((dq, dk, dv)):
            r["dpacked"][i, :, live] = v[:, :width].astype(BF)
    sums = [col_sum(r["dpacked"][i].astype(F32)) for i in (0, 2)]
    sums = jnp.concatenate(sums + [jnp.zeros((14, D), F32)], axis=0).astype(BF)
    r["small"][2:4] = matmul(sums, order[:D])[:2]
    r["acc"][...] = jnp.zeros((ROWS, PAD), F32)

    def project(i, carry):
        if wait:
            w.wait(QKV + i)
        r["acc"][:, :D] += dot_t(r["dpacked"][i], w.buf[QKV + i, :, :D])
        return carry

    lax.fori_loop(0, 3, project, 0)
    dentry = r["acc"][:, :D]
    normed, inverse = norm_parts(x_ref[...].astype(F32))
    r["small"][0:1] = col_sum(dentry * normed)
    r["small"][1:2] = col_sum(dentry)
    r["small"][12:16] = jnp.zeros((4, D), F32)
    r["dx"][...] = (r["middle"][...] + norm_back(dentry, normed, inverse, vecs[0:1])).astype(BF)


ROW = (ROWS, D)
KEPT = {
    "packed": ((3, ROWS, PAD), BF),
    "middle": (ROW, F32),
    "hidden": ((4,) + ROW, F32),
}
FWD_OUT = {
    "result": (ROW, BF),
    "entry": (ROW, BF),
    "mixed": (ROW, BF),
    "second": (ROW, BF),
    "active": ((4,) + ROW, BF),
}
BWD_OUT = {
    "dx": (ROW, BF),
    "dhidden": ((4,) + ROW, BF),
    "dpacked": ((4,) + ROW, BF),
    "small": ((16, D), F32),
}
WORK = {"heads": ((ROWS, PAD), BF), "acc": ((ROWS, PAD), F32)}


def layer_call(kind, whole, tails, vecs, nat, pairs, order, x, grad=None, kept=None):
    outs = dict(FWD_OUT) if kind != "bwd" else {}
    if kind == "fwd":
        outs.update(KEPT)
    else:
        outs.update(BWD_OUT)
    work = dict(WORK)
    if kind == "both":
        work.update(KEPT)
    if kind == "bwd":
        work["middle"] = KEPT["middle"]
    ins = [whole, tails, vecs, nat, pairs, order, x]
    if grad is not None:
        ins.append(grad)
    if kind == "bwd":
        ins += [kept["packed"], kept["middle"], kept["hidden"]]

    def kernel(*refs):
        given, refs = refs[: len(ins)], refs[len(ins) :]
        out_refs, refs = refs[: len(outs)], refs[len(outs) :]
        r = dict(zip(outs, out_refs))
        r.update(zip(work, refs))
        buf, sems = refs[len(work) :]
        w = Weights(given[0], given[1], buf, sems)
        vecs_ref, nat_ref, pairs_ref, order_ref, x_ref = given[2:7]
        if kind == "bwd":
            blocks = [b for a in range(4) for b in (DOWN + a, UP + a)] + [OUT, 8, 9, 10]
            w.start(blocks)
            r["packed"], r["hidden"] = given[8], given[10]
            r["middle"][...] = given[9][...]
            backward_part(w, True, given[7], x_ref, pairs_ref, vecs_ref, order_ref, r)
            return
        w.start([8, 9, 10, OUT] + [b for a in range(4) for b in (UP + a, DOWN + a)])
        forward_part(w, True, x_ref, pairs_ref, vecs_ref, nat_ref, order_ref, r)
        if kind == "both":
            backward_part(w, False, given[7], x_ref, pairs_ref, vecs_ref, order_ref, r)

    vm = pl.BlockSpec(memory_space=pltpu.VMEM)
    hbm = pl.BlockSpec(memory_space=pl.ANY)
    results = pl.pallas_call(
        kernel,
        in_specs=[hbm, hbm] + [vm] * (len(ins) - 2),
        out_specs=[vm] * len(outs),
        out_shape=[jax.ShapeDtypeStruct(s, t) for s, t in outs.values()],
        scratch_shapes=[pltpu.VMEM(s, t) for s, t in work.values()]
        + [pltpu.VMEM((BLOCKS, D, PAD), BF), pltpu.SemaphoreType.DMA((BLOCKS, 2))],
        compiler_params=pltpu.CompilerParams(vmem_limit_bytes=VMEM_BYTES),
        name="layer_" + kind,
    )(*ins)
    return dict(zip(outs, results))


def zeros_of(spec):
    return {name: jnp.zeros(s, t) for name, (s, t) in spec.items()}


def pad_cols(v, width):
    return jnp.pad(v, ((0, 0), (0, width - v.shape[1])))


def body(inputs, cotangent, lengths, vectors, qkv_w, out_w, up_w, up_b, down_w):
    section = lax.axis_index("section")
    zi = lax.axis_index("z")
    mb, rows, _ = inputs.shape
    n = mb * rows
    c = constants()
    order = c["order"]

    outdown = matmul(jnp.concatenate([out_w[0], down_w[0]], axis=0), order[:D]).astype(BF)
    hid = matmul(up_w[0].reshape(SHARD * 4, D), c["hid"]).astype(BF).reshape(SHARD, 4, D)
    hid_main = hid[:, :, :MAIN].reshape(SHARD, 4, 4, 256).transpose(0, 2, 1, 3)
    hid_last = hid[:, :, MAIN:].reshape(SHARD, 4, 4, 16).transpose(0, 2, 1, 3)
    hid = jnp.concatenate(
        [
            hid_main.reshape(SHARD, 4, MAIN),
            hid_last.reshape(SHARD, 4, NDP),
            jnp.zeros((SHARD, 4, PAD - D), BF),
        ],
        axis=2,
    )
    shard = [hid.reshape(SHARD, 4 * PAD)]
    shard += [pad_cols(outdown[SHARD * (1 + a) : SHARD * (2 + a)], PAD) for a in range(4)]
    shard += [pad_cols(qkv_w[0][:, i * D : (i + 1) * D], PAD) for i in range(3)]
    shard += [pad_cols(outdown[:SHARD], PAD)]
    shard = jnp.concatenate(shard, axis=1)
    tail = jnp.concatenate([shard[16], vectors[0].reshape(-1), up_b[0]])
    tail = jnp.pad(tail, (0, 16 * TAILW - tail.shape[0])).reshape(16, TAILW)
    sent = jnp.concatenate([shard[:16], tail], axis=1)
    whole = lax.all_gather(sent, ("x", "y", "z"), axis=0, tiled=True)
    tails, vecs, nat = unpack(whole, c)

    ends = jnp.cumsum(lengths[:, 0], axis=1)
    place = jnp.arange(rows, dtype=jnp.int32)
    seg = jnp.sum((place[None, :, None] >= ends[:, None, :]).astype(jnp.int32), axis=2)
    seg = (seg + 8 * jnp.arange(mb, dtype=jnp.int32)[:, None]).reshape(n)
    at = jnp.arange(n, dtype=jnp.int32)
    pairs = ((seg[:, None] == seg[None, :]) & (at[:, None] >= at[None, :])).astype(F32)

    x0 = matmul(inputs.reshape(n, D), order[:D]).astype(BF)
    cot = matmul(cotangent.reshape(n, D), order[:D]).astype(BF)
    call = functools.partial(
        layer_call, whole=whole, tails=tails, vecs=vecs, nat=nat, pairs=pairs, order=order
    )

    first = lax.cond(
        section == 0,
        lambda: call("fwd", x=x0),
        lambda: zeros_of({**FWD_OUT, **KEPT}),
    )
    arrived = lax.ppermute(first["result"], "section", [(0, 1)])
    kept = {k: first[k] for k in KEPT}
    fwd = {k: first[k] for k in FWD_OUT}

    def top():
        out = call("both", x=arrived, grad=cot)
        return {k: out[k] for k in FWD_OUT}, {k: out[k] for k in BWD_OUT}

    fwd, bwd = lax.cond(section == 1, top, lambda: (fwd, zeros_of(BWD_OUT)))
    coming = lax.ppermute(bwd["dx"], "section", [(1, 0)])
    bwd = lax.cond(
        section == 0, lambda: call("bwd", x=x0, grad=coming, kept=kept), lambda: bwd
    )
    dbranch = jnp.where(section == 0, coming, cot)

    entry = fwd["entry"]
    blocks = jnp.stack(
        [
            jnp.stack([entry, entry, entry, fwd["mixed"]]),
            bwd["dpacked"],
            fwd["active"],
            bwd["dhidden"],
        ]
    )

    def for_z(target):
        own = lax.dynamic_index_in_dim(blocks, target, 1, keepdims=False)
        return jnp.concatenate([own, fwd["second"][None], dbranch[None]], axis=0)

    parts = [for_z(zi)]
    for d in (1, 2, 3):
        parts.append(
            lax.ppermute(for_z((zi + d) % 4), "z", [(i, (i + d) % 4) for i in range(4)])
        )
    a_attn, b_attn, act_z, dhid_z, sec_all, db_all = jnp.concatenate(parts, axis=1)
    wgrads = ((sec_all, dhid_z), (act_z, db_all), (a_attn, b_attn))
    wide = 3 * D + 64

    main = jnp.concatenate([t_dot(a[:, :MAIN], b).astype(BF) for a, b in wgrads], axis=1)
    last = jnp.concatenate([t_dot(a[:, MAIN:], b).astype(BF) for a, b in wgrads], axis=1)
    small = pad_cols(bwd["small"].T.astype(BF), 64)
    main = jnp.concatenate([main, small[:MAIN]], axis=1).reshape(16, 64, wide)
    last = jnp.concatenate([last, small[MAIN:]], axis=1).reshape(16, 4, wide)
    payload = jnp.concatenate([main, last, jnp.zeros((16, 4, wide), BF)], axis=1)
    payload = lax.optimization_barrier(payload.reshape(16 * 72, wide))
    got = lax.psum_scatter(payload, ("x", "y"), scatter_dimension=0, tiled=True)
    got = lax.optimization_barrier(got)
    to_z = jnp.concatenate(
        [got[:64].reshape(4, 16, wide), got[64:68].reshape(4, 1, wide), jnp.zeros((4, 7, wide), BF)],
        axis=1,
    )
    mine = lax.all_to_all(to_z, "z", 0, 0, tiled=True)[:, :SHARD]

    g_hid = mine[:, :, :D].transpose(1, 0, 2)
    g_main = g_hid[:, :, :MAIN].reshape(SHARD, 4, 4, 256).transpose(0, 2, 1, 3)
    g_last = g_hid[:, :, MAIN:].reshape(SHARD, 4, 4, 16).transpose(0, 2, 1, 3)
    g_hid = jnp.concatenate(
        [g_main.reshape(SHARD, 4, MAIN), g_last.reshape(SHARD, 4, NDP)], axis=2
    )
    g_up = dot_t(g_hid.reshape(SHARD * 4, D), c["hid"]).reshape(SHARD, FF)
    cols = jnp.concatenate(
        [mine[:, :, D : 2 * D].reshape(4 * SHARD, D), mine[3, :, 2 * D : 3 * D]], axis=0
    )
    cols = dot_t(cols, order[:D])
    g_qkv = mine[:3, :, 2 * D : 3 * D].transpose(1, 0, 2).reshape(SHARD, 3 * D).astype(F32)
    sums = jnp.sum(mine[:, :, 3 * D : 3 * D + 12].astype(F32), axis=0)
    back = dot_t(jnp.concatenate([fwd["result"], bwd["dx"]], axis=0), order[:D]).astype(BF)
    return (
        back[:n].reshape(1, mb, rows, D),
        back[n:].reshape(1, mb, rows, D),
        sums[None, :, :8],
        g_qkv[None],
        cols[None, 4 * SHARD :],
        g_up[None],
        sums[:, 8:].T.reshape(1, 4 * SHARD),
        cols[None, : 4 * SHARD],
    )


def solution(mesh):
    grid = Mesh(mesh.devices.reshape(2, 4, 4, 4), ("section", "x", "y", "z"))
    dp = ("x", "y", "z")
    tokens = P(None, dp, None)
    rows = P("section", dp, None)
    in_specs = (tokens, tokens, tokens, rows, rows, rows, rows, P("section", dp), rows)
    stacks = P("section", None, dp, None)
    out_specs = (stacks, stacks, rows, rows, rows, rows, P("section", dp), rows)
    return jax.shard_map(body, mesh=grid, in_specs=in_specs, out_specs=out_specs, check_vma=False)
```

time: 732 us -> 490 us (0.67)
  waiting for transfers between devices: 428 us -> 306 us
  matrix products: 99.3 us -> 19.9 us
  local copies, waits for them, and re-layouts: 119 us -> 52.4 us
  Pallas kernels: 0 us -> 45.2 us
  other arithmetic: 47.7 us -> 29.7 us
    ppermute x2, waiting for transfers between devices: 109 us -> 25.6 us  [the longest x1 25.6 us: body(): coming = lax.ppermute(bwd['dx'], 'section', [(1, 0)])]
    unnamed x3, waiting for transfers between devices: 130 us -> 82.4 us
    pallas_call x0 -> x3, Pallas kernels: none -> 45.2 us  [the longest x2 37.8 us: layer_call(): pl.pallas_call(kernel, in_specs=[hbm, hbm] + [vm] * (len(ins) - 2), out_s...]
    slice x29 -> x14, local copies, waits for them, and re-layouts: 50.4 us -> 6.57 us  [the longest x2 2.68 us: body(): back[n:].reshape(1, mb, rows, D)]
    dot_general x19 -> x4, matrix products: 44.5 us -> 7.85 us  [matmul(): return jnp.dot(a, b, preferred_element_type=F32)]
    dot_general x17 -> x4, matrix products: 35.7 us -> 6.58 us  [dot_t(): lax.dot_general(a, b, (((1,), (1,)), ((), ())), preferred_element_type=F32)]
    reduce_sum x7 -> x0, other arithmetic: 11.4 us -> none  [the longest x2 8.47 us: total(): return jnp.sum(v.astype(F32), axis=0)]
    dot_general x6 -> x0, matrix products: 9.99 us -> none  [the longest x1 2.48 us: backward(): jnp.einsum('hqk,qhd->khd', soft.astype(BF), dm, preferred_element_type=F32)]
  transfers between devices with their start and end apart: 8 -> 8, of which waited for: 7 -> 7; matrix products, arithmetic and copies ran while one was open for 3% -> 4% of each run, Pallas kernels for 0% -> 0%
where the time goes in v2:
time: 490 us; the launch traced here: 481 us
  waiting for transfers between devices  306 us (62%)
  local copies, waits for them, and re-layouts  52.4 us (11%)
  Pallas kernels  45.2 us (9%)
  other arithmetic  29.7 us (6%)
  matrix products  19.9 us (4%)
  between operations  15.1 us (3%)
  starting transfers between devices  12.3 us (3%)
    all_gather x1, waiting for transfers between devices, body(): whole = lax.all_gather(sent, ('x', 'y', 'z'), axis=0, tiled=True)  148 us
    unnamed x3, waiting for transfers between devices  82.4 us
    ppermute x3, waiting for transfers between devices, body(): lax.ppermute(for_z((zi + d) % 4), 'z', [(i, (i + d) % 4) for i in range(4)])  44.2 us
    pallas_call x2, Pallas kernels, layer_call(): pl.pallas_call(kernel, in_specs=[hbm, hbm] + [vm] * (len(ins) - 2), out_s...  37.8 us
    ppermute x1, waiting for transfers between devices, body(): coming = lax.ppermute(bwd['dx'], 'section', [(1, 0)])  25.6 us
    concatenate x1, local copies, waits for them, and re-layouts, body(): main = jnp.concatenate([main, small[:MAIN]], axis=1).reshape(16, 64, wide)  9.94 us
  transfers between devices with their start and end apart: 8, of which 7 were waited for; matrix products, arithmetic and copies ran while one was open for 4% of the time, Pallas kernels for 0%

profile of v2, /device:TPU:0, one launch (start us, length us, event | category | flops | bytes accessed | tf_op | source)
XLA Modules:
  0.0 480.8 jit_solution(13443716077061651509)
XLA Ops:
  20.1 148.3 %all-gather.2.cloned.1.call-done.whole = bf16[1024,14720]{1,0:T(8,128)(2,1)} async-done(((bf16[16,14720]{1,0:T(8,128)(2,1)}), bf16[1024,14720]{1,0:T(8,128)(2,1)}) %all-gather.2.cloned.1.call-update) | async-done | bytes 30146576 | tf_op jit(solution)/shard_map/all_gather | solution.py:410
  168.4 7.4 %unpack.1 = (bf16[64,14336]{1,0:T(8,128)(2,1)}, f32[16,1088]{1,0:T(8,128)}, f32[16,1152]{1,0:T(8,128)}) custom-call(bf16[1024,14720]{1,0:T(8,128)(2,1)} %all-gather.2.cloned.1.call-done.whole, bf16[16,256]{1,0:T(8,128)(2,1)} %constant.91.clone.pick, bf16[64,1088]{1,0:T(8,128)(2,1)} %constant.92.clone.spread, bf16[256,1088]{1,0:T(8,128)(2,1)} %constant.93.clone.keep, ...), custom_call_target="tpu_custom_call" | custom-call | tf_op jit(solution)/shard_map/unpack/pallas_call | solution.py:108
  175.8 15.3 %conditional.3 = (bf16[4,128,1088]{2,1,0:T(8,128)(2,1)}, bf16[128,1088]{1,0:T(8,128)(2,1)}, f32[4,128,1088]{2,1,0:T(8,128)}, f32[128,1088]{1,0:T(8,128)S(1)}, bf...) conditional(s32[]{:T(128)} %convert_element_type.85, () %tuple.38, ...), branch_computations={%region_2.3_spmd, %region_3.4_spmd} | conditional | bytes 5898324 | solution.py:426
  176.7 14.3 %layer_fwd.1 = (bf16[128,1088]{1,0:T(8,128)(2,1)}, bf16[128,1088]{1,0:T(8,128)(2,1)}, bf16[128,1088]{1,0:T(8,128)(2,1)}, bf16[128,1088]{1,0:T(8,128)(2,1)}, bf16...) custom-call(bf16[1024,14720]{1,0:T(8,128)(2,1)} %get-tuple-element.8, ...), custom_call_target="tpu_custom_call" | custom-call | tf_op jit(solution)/shard_map/cond/branch_1_fun/layer_fwd/pallas_call | solution.py:361
  192.4 3.3 fusion.1
  195.7 3.0 conditional.4
  202.1 2.6 maximum_bitcast_fusion
  204.6 25.6 %collective-permute-done.1 = bf16[128,1088]{0,1:T(8,128)(2,1)} collective-permute-done((bf16[128,1088]{0,1:T(8,128)(2,1)}, bf16[128,1088]{0,1:T(8,128)(2,1)}, u32[]{:S(2)}, u32[]{:S(2)}) %collective-permute-start.1) | collective-permute-done | bytes 278560 | tf_op jit(solution)/shard_map/ppermute | solution.py:440
  230.2 27.3 %conditional.5 = (bf16[128,1088]{1,0:T(8,128)(2,1)}, f32[16,1088]{1,0:T(8,128)}, bf16[1,4,128,1088]{3,2,1,0:T(8,128)(2,1)}, bf16[1,4,128,1088]{3,2,1,0:T(8,128)(2,1)}) conditional(s32[]{:T(128)} %convert_element_type.85, (bf16[128,1088]{1,0:T(8,128)(2,1)}, f32[16,1088]{1,0:T(8,128)}, bf16[4,128,1088]{2,1,0:T(8,128)(2,1)}, ...), branch_computations={%region_6.7_spmd, %region_7.8_spmd} | conditional | bytes 1114144 | solution.py:441
  234.1 23.4 %layer_bwd.1 = (bf16[128,1088]{1,0:T(8,128)(2,1)}, bf16[4,128,1088]{2,1,0:T(8,128)(2,1)}, bf16[4,128,1088]{2,1,0:T(8,128)(2,1)}, f32[16,1088]{1,0:T(8,128)}) custom-call(bf16[1024,14720]{1,0:T(8,128)(2,1)} %get-tuple-element.117.refs_0_, bf16[64,14336]{1,0:T(8,128)(2,1)} %get-tuple-element.118.refs_1_, f32[16,1088]{1,0:T(8,128)} %get-tuple-element.119.refs_2_, ...), custom_call_target="tpu_custom_call" | custom-call | tf_op jit(solution)/shard_map/cond/branch_1_fun/layer_bwd/pallas_call | solution.py:361
  257.5 2.7 pad_maximum_fusion.2
  264.6 2.4 copy.159
  269.4 3.9 pad_maximum_fusion.5
  274.2 2.9 collective-permute-start.3
  280.5 26.1 %collective-permute-done.2 = bf16[6,128,1088]{1,2,0:T(8,128)(2,1)} collective-permute-done((bf16[6,128,1088]{1,2,0:T(8,128)(2,1)}, bf16[6,128,1088]{1,2,0:T(8,128)(2,1)}, u32[]{:S(2)}, u32[]{:S(2)}) %collective-permute-start.2) | collective-permute-done | bytes 1671200 | tf_op jit(solution)/shard_map/ppermute | solution.py:463
  306.6 17.9 %collective-permute-done.3 = bf16[6,128,1088]{1,2,0:T(8,128)(2,1)} collective-permute-done((bf16[6,128,1088]{1,2,0:T(8,128)(2,1)}, bf16[6,128,1088]{1,2,0:T(8,128)(2,1)}, u32[]{:S(2)}, u32[]{:S(2)}) %collective-permute-start.3) | collective-permute-done | bytes 1671200 | tf_op jit(solution)/shard_map/ppermute | solution.py:463
  324.7 3.9 pad_maximum_fusion.1
  334.3 3.6 pad_maximum_fusion
  337.9 9.9 %copy.161 = bf16[1024,3328]{1,0:T(8,128)(2,1)} copy(bf16[1024,3328]{0,1:T(8,128)(2,1)} %pad_maximum_fusion) | data formatting | bytes 13631488 | tf_op jit(solution)/shard_map/concatenate | solution.py:472
  348.1 7.5 %maximum_maximum_fusion = bf16[16,72,3328]{2,1,0:T(8,128)(2,1)} fusion(bf16[16,4,3328]{2,1,0:T(4,128)(2,1)S(1)} %reshape.139, bf16[16,64,3328]{2,1,0:T(8,128)(2,1)} %bitcast.102, bf16[72]{0:T(256)(128)(2,1)S(1)} %pad.50.clone), kind=kLoop, calls=%fused_computation | loop fusion | flops 23003136 | bytes 14909584 | tf_op jit(solution)/shard_map/concatenate | solution.py:474
  357.3 2.8 convolution_convert_fusion.3
  360.1 82.4 %reduce-scatter.4.cloned.1.call-done = bf16[72,3328]{1,0:T(8,128)(2,1)} async-done(((bf16[1152,3328]{1,0:T(8,128)(2,1)}), bf16[72,3328]{1,0:T(8,128)(2,1)}) %reduce-scatter.4.cloned.1.call-update) | async-done | bytes 479248
  445.3 4.4 all-to-all-start
  454.2 5.4 %all-to-all-done = bf16[4,24,3328]{2,1,0:T(8,128)(2,1)S(1)} async-done(((bf16[4,24,3328]{2,1,0:T(8,128)(2,1)}), bf16[4,24,3328]{2,1,0:T(8,128)(2,1)S(1)}, u32[]{:S(2)}, u32[]{:S(2)}) %all-to-all-start) | async-done | bytes 639008 | tf_op jit(solution)/shard_map/all_to_all | solution.py:482
  (152 shorter events, 64.7 us)
Async XLA Ops:
  7.2 11.4 %copy-start = (bf16[2,64,1088]{2,1,0:T(8,128)(2,1)S(1)}, bf16[2,64,1088]{2,1,0:T(8,128)(2,1)}, u32[]{:S(2)}) copy-start(bf16[2,64,1088]{2,1,0:T(8,128)(2,1)} %param.23) | copy-start | bytes 835588
  7.2 161.2 %all-gather.2.cloned.1.call-start = ((), (), s32[]{:S(2)}) async-start(), calls=%async_computation.2 | async-start | bytes 30617600 | tf_op jit(solution)/shard_map/all_gather | solution.py:410
  8.4 2.6 copy-start.3
  8.4 2.6 copy-start.14
  8.4 2.6 copy-start.15
  11.0 3.3 copy-start.13
  11.6 2.9 copy-start.16
  11.7 3.1 copy-start.17
  16.6 425.8 %reduce-scatter.4.cloned.1.call-start = ((), (), s32[]{:S(2)}) async-start(), calls=%async_computation.3 | async-start | bytes 8146944
  20.1 155.6 %copy-start.2 = (bf16[1152,1088]{1,0:T(8,128)(2,1)S(1)}, bf16[1152,1088]{1,0:T(8,128)(2,1)}, u32[]{:S(2)}) copy-start(bf16[1152,1088]{1,0:T(8,128)(2,1)} %constant.89.clone) | copy-start | bytes 7520260
  20.1 155.7 %copy-start.8 = (bf16[128,1088]{0,1:T(8,128)(2,1)S(1)}, bf16[128,1088]{0,1:T(8,128)(2,1)}, u32[]{:S(2)}) copy-start(bf16[128,1088]{0,1:T(8,128)(2,1)} %fusion) | copy-start | bytes 835588
  191.1 4.6 collective-permute-start
  198.7 2.2 copy-start.6
  199.6 30.6 %collective-permute-start.1 = (bf16[128,1088]{0,1:T(8,128)(2,1)}, bf16[128,1088]{0,1:T(8,128)(2,1)}, u32[]{:S(2)}, u32[]{:S(2)}) collective-permute-start(bf16[128,1088]{0,1:T(8,128)(2,1)} %copy.151), channel_id=1, source_target_pairs={{64,0},{65,1},{66,2},{67,3},{68,4},{69,5},{70,6},{71,7},{72,8},{73... | collective-permute-start | bytes 835592 | tf_op jit(solution)/shard_map/ppermute | solution.py:440
  264.6 3.9 copy-start.9
  273.3 33.3 %collective-permute-start.2 = (bf16[6,128,1088]{1,2,0:T(8,128)(2,1)}, bf16[6,128,1088]{1,2,0:T(8,128)(2,1)}, u32[]{:S(2)}, u32[]{:S(2)}) collective-permute-start(bf16[6,128,1088]{1,2,0:T(8,128)(2,1)} %get-tuple-element.407), channel_id=1, source_target_pairs={{0,1},{1,2},{2,3},{3,0},{4,5},{5,6},{6,7},{7,4},{8,9},{9,10},{10,1... | collective-permute-start | bytes 5013512 | tf_op jit(solution)/shard_map/ppermute | solution.py:463
  274.2 50.4 %collective-permute-start.3 = (bf16[6,128,1088]{1,2,0:T(8,128)(2,1)}, bf16[6,128,1088]{1,2,0:T(8,128)(2,1)}, u32[]{:S(2)}, u32[]{:S(2)}) collective-permute-start(bf16[6,128,1088]{1,2,0:T(8,128)(2,1)} %get-tuple-element.408), channel_id=1, source_target_pairs={{0,2},{1,3},{2,0},{3,1},{4,6},{5,7},{6,4},{7,5},{8,10},{9,11},{10,... | collective-permute-start | bytes 5013512 | tf_op jit(solution)/shard_map/ppermute | solution.py:463
  277.0 47.7 %collective-permute-start.4 = (bf16[6,128,1088]{1,2,0:T(8,128)(2,1)}, bf16[6,128,1088]{1,2,0:T(8,128)(2,1)}, u32[]{:S(2)}, u32[]{:S(2)}) collective-permute-start(bf16[6,128,1088]{1,2,0:T(8,128)(2,1)} %get-tuple-element.409), channel_id=1, source_target_pairs={{0,3},{1,0},{2,1},{3,2},{4,7},{5,4},{6,5},{7,6},{8,11},{9,8},{10,9... | collective-permute-start | bytes 5013512 | tf_op jit(solution)/shard_map/ppermute | solution.py:463
  355.6 1.7 copy-start.7
  445.3 14.3 %all-to-all-start = ((bf16[4,24,3328]{2,1,0:T(8,128)(2,1)}), bf16[4,24,3328]{2,1,0:T(8,128)(2,1)S(1)}, u32[]{:S(2)}, u32[]{:S(2)}) async-start(bf16[4,24,3328]{2,1,0:T(8,128)(2,1)} %maximum_maximum_fusion.1), calls=%async_computation | async-start | bytes 1277952 | tf_op jit(solution)/shard_map/all_to_all | solution.py:482
  461.2 2.8 copy-start.10
  463.1 2.1 copy-start.5
  465.1 1.8 copy-start.12
  465.2 8.4 %copy-start.1 = (bf16[2,64,1088]{2,1,0:T(8,128)(2,1)S(1)}, bf16[2,64,1088]{2,1,0:T(8,128)(2,1)}, u32[]{:S(2)}) copy-start(bf16[2,64,1088]{2,1,0:T(8,128)(2,1)} %param.23) | copy-start | bytes 835588
  (1 other events, 1.7 us)
Sparse Core Ops, SparseCore 0:
  16.8 151.5 all-gather.1
  355.7 86.6 reduce-scatter.3
